TPU v7x, 256 devices: a whole 4x4x8 slice. The times are simulated.
256 devices in a mesh: orb: 32 (over y, x, core), aux: 8 (over z).
Axes of the slice: x: 4, y: 4, z: 8, core: 2. Of those that a mesh axis runs over, the one named last changes fastest.
Arguments:
- coulomb_blocks: bfloat16 [256, 768, 768], P(None, 'orb'), may hold values from -0.21875 to 0.21875
- occupancy: int32 [96, 96], P('orb'), may hold values 0 or 1
- green_occ: bfloat16 [768, 768], replicated, may hold values from -0.21875 to 0.21875
- green_virt: bfloat16 [768, 768], P(None, 'aux'), may hold values from -0.21875 to 0.21875
Outputs:
- polarizability: float32 [256, 256], P('aux', 'orb')
All inputs are finite; a program needn't handle non-finite values. No bound on the sum of `occupancy` on one device may be relied on, other than what follows from the above.
Results may differ from a plain program's by a relative error of at most 0.0041.
Values may be sent and summed in bfloat16 or wider, within the bound.
No kernel may reach another device: no remote copies, remote signals or barrier semaphores. Data moves between devices by JAX's collectives and lax.ppermute only.
A program may use at most 128 MiB of HBM per device.

v0:
```python
import jax
import jax.numpy as jnp
from jax import lax
from jax.sharding import PartitionSpec as P

BLK = 8


def shards(coulomb_blocks, occupancy, green_occ, green_virt):
    naux = coulomb_blocks.shape[0]
    mu_rows = coulomb_blocks.shape[1]
    nao = coulomb_blocks.shape[2]
    sig_cols = green_virt.shape[1]
    mask = jnp.repeat(jnp.repeat(occupancy, BLK, 0), BLK, 1).astype(jnp.bfloat16)
    screened = coulomb_blocks * mask[None, :, :]
    own_cols = lax.dynamic_slice_in_dim(screened, lax.axis_index("aux") * sig_cols, sig_cols, 2)
    half_virt = jnp.dot(
        screened.reshape(naux * mu_rows, nao), green_virt, preferred_element_type=jnp.float32
    )
    half_virt = half_virt.astype(jnp.bfloat16).reshape(naux, mu_rows, sig_cols)
    aux_major = lax.all_to_all(half_virt, "orb", split_axis=0, concat_axis=1, tiled=True)
    both_sides = jnp.einsum("lm,pms->pls", green_occ, aux_major, preferred_element_type=jnp.float32)
    both_sides = both_sides.astype(jnp.bfloat16)
    returned = lax.all_to_all(both_sides, "orb", split_axis=1, concat_axis=0, tiled=True)
    partial_pol = jnp.dot(
        returned.reshape(naux, mu_rows * sig_cols),
        own_cols.reshape(naux, mu_rows * sig_cols).T,
        preferred_element_type=jnp.float32,
    )
    row_share = lax.psum_scatter(partial_pol, "aux", scatter_dimension=0, tiled=True)
    result = lax.psum_scatter(row_share, "orb", scatter_dimension=1, tiled=True)
    return result


def solution(mesh):
    in_specs = (P(None, "orb", None), P("orb", None), P(), P(None, "aux"))
    out_specs = P("aux", "orb")
    return jax.shard_map(shards, mesh=mesh, in_specs=in_specs, out_specs=out_specs, check_vma=False)
```

profile of v0, /device:TPU:1, one launch (start us, length us, event | category | flops | bytes accessed | tf_op | source)
XLA Modules:
  0.0 254.1 jit_solution(4675063912139333811)
XLA Ops:
  6.5 0.0 copy-start
  6.5 0.8 convert_element_type.24
  7.3 0.1 copy.25
  7.5 0.1 copy.26
  7.6 0.0 copy-start.2
  7.6 8.0 %broadcast_multiply_fusion = bf16[256,24,768]{2,1,0:T(8,128)(2,1)} fusion(bf16[256,24,768]{2,1,0:T(8,128)(2,1)} %param.4, bf16[24,768]{1,0:T(8,128)(2,1)S(1)} %copy.26), kind=kLoop, calls=%fused_computation.1 | loop fusion | flops 4718592 | bytes 18911232 | tf_op jit(solution)/shard_map/mul | solution.py:15
  15.6 0.0 copy-done.2
  15.6 6.6 %convolution_convert_fusion = bf16[6144,96]{0,1:T(8,128)(2,1)S(1)} fusion(bf16[6144,768]{1,0:T(8,128)(2,1)} %bitcast.29, bf16[768,96]{0,1:T(8,128)(2,1)S(1)} %copy-done.2), kind=kOutput, calls=%fused_computation | convolution fusion | flops 906559488 | bytes 10764288 | tf_op jit(solution)/shard_map/dot_general | solution.py:17
  22.2 1.6 copy.27
  23.8 31.4 %all_to_all.33 = bf16[256,24,96]{2,1,0:T(8,128)(2,1)S(1)} all-to-all(bf16[256,24,96]{2,1,0:T(8,128)(2,1)} %bitcast.32), channel_id=1, replica_groups=mesh['orb'=32,'aux'=8] {'orb'}, dimensions={0} | all-to-all | bytes 2359296 | tf_op jit(solution)/shard_map/all_to_all | solution.py:21
  55.2 0.3 copy.28
  55.4 0.0 copy-done
  55.5 1.5 fusion
  57.0 2.0 copy.30
  58.9 4.1 %all-to-all-start.1 = ((bf16[8,768,96]{2,0,1:T(8,128)(2,1)}), bf16[8,768,96]{2,0,1:T(8,128)(2,1)S(1)}, u32[]{:S(2)}, u32[]{:S(2)}) async-start(bf16[8,768,96]{2,0,1:T(8,128)(2,1)} %copy.30), calls=%async_computation.1 | async-start | bytes 3145728 | tf_op jit(solution)/shard_map/all_to_all | solution.py:24
  63.0 0.0 reduce-scatter.3.cloned.1.call-start
  63.1 3.6 %constant_dynamic-slice_fusion.1 = bf16[256,24,96]{2,1,0:T(8,128)(2,1)} fusion(bf16[256,24,768]{2,1,0:T(8,128)(2,1)} %broadcast_multiply_fusion, s32[]{:T(128)S(6)} %select_n.3), kind=kLoop, calls=%fused_computation.8 | loop fusion | bytes 2359300 | tf_op jit(solution)/shard_map/dynamic_slice | solution.py:16
  66.7 2.8 %copy.33 = bf16[256,24,96]{0,2,1:T(8,128)(2,1)} copy(bf16[256,24,96]{2,1,0:T(8,128)(2,1)} %constant_dynamic-slice_fusion.1) | data formatting | bytes 2359296 | tf_op jit(solution)/shard_map/dynamic_slice | solution.py:16
  69.5 15.8 %all-to-all-done.1 = bf16[8,768,96]{2,0,1:T(8,128)(2,1)S(1)} async-done(((bf16[8,768,96]{2,0,1:T(8,128)(2,1)}), bf16[8,768,96]{2,0,1:T(8,128)(2,1)S(1)}, u32[]{:S(2)}, u32[]{:S(2)}) %all-to-all-start.1) | async-done | bytes 1179680 | tf_op jit(solution)/shard_map/all_to_all | solution.py:24
  85.3 1.5 copy.32
  86.8 0.0 copy-start.1
  86.8 3.0 %reshape.24 = bf16[256,2304]{1,0:T(8,128)(2,1)S(1)} reshape(bf16[32,8,24,96]{3,2,1,0:T(8,128)(2,1)} %copy.32) | data formatting | bytes 2359296 | tf_op jit(solution)/shard_map/reshape | solution.py:26
  89.8 0.0 copy-start.3
  89.8 0.0 copy-done.1
  89.8 1.2 fusion.2
  90.9 0.0 reduce-scatter.3.cloned.1.call-update
  91.0 0.0 copy-done.3
  91.0 0.6 dynamic-slice
  92.2 30.0 %reduce-scatter.3.cloned.1.call-done = f32[32,256]{1,0:T(8,128)} async-done(((f32[256,256]{1,0:T(8,128)}), f32[32,256]{1,0:T(8,128)}) %reduce-scatter.3.cloned.1.call-update) | async-done | bytes 32784 | tf_op jit(solution)/shard_map/reduce_scatter | solution.py:30
  122.2 124.3 %all-reduce = f32[32,256]{1,0:T(8,128)S(1)} all-reduce(f32[32,256]{1,0:T(8,128)} %reduce-scatter.3.cloned.1.call-done), channel_id=3, replica_groups=mesh['orb'=32,'aux'=8] {'orb'}, use_global_device_ids=true, to_apply=%region_1.0.clone | all-reduce | flops 8192 | bytes 65536
  246.5 0.1 constant_dynamic-slice_fusion
  246.6 0.7 copy.34
  (2 shorter events, 0.0 us)
Async XLA Ops:
  6.5 48.9 %copy-start = (bf16[768,768]{1,0:T(8,128)(2,1)S(1)}, bf16[768,768]{1,0:T(8,128)(2,1)}, u32[]{:S(2)}) copy-start(bf16[768,768]{1,0:T(8,128)(2,1)} %param.6) | copy-start | bytes 3538948
  7.6 8.0 %copy-start.2 = (bf16[768,96]{0,1:T(8,128)(2,1)S(1)}, bf16[768,96]{0,1:T(8,128)(2,1)}, u32[]{:S(2)}) copy-start(bf16[768,96]{0,1:T(8,128)(2,1)} %param.7) | copy-start | bytes 442372
  58.9 26.3 %all-to-all-start.1 = ((bf16[8,768,96]{2,0,1:T(8,128)(2,1)}), bf16[8,768,96]{2,0,1:T(8,128)(2,1)S(1)}, u32[]{:S(2)}, u32[]{:S(2)}) async-start(bf16[8,768,96]{2,0,1:T(8,128)(2,1)} %copy.30), calls=%async_computation.1 | async-start | bytes 3145728 | tf_op jit(solution)/shard_map/all_to_all | solution.py:24
  63.0 59.2 %reduce-scatter.3.cloned.1.call-start = ((), (), s32[]{:S(2)}) async-start(), calls=%async_computation.3 | async-start | bytes 294912 | tf_op jit(solution)/shard_map/reduce_scatter | solution.py:30
  86.8 3.0 %copy-start.1 = (bf16[256,24,96]{0,2,1:T(8,128)(2,1)S(1)}, bf16[256,24,96]{0,2,1:T(8,128)(2,1)}, u32[]{:S(2)}) copy-start(bf16[256,24,96]{0,2,1:T(8,128)(2,1)} %copy.33) | copy-start | bytes 3538948
  89.8 1.2 copy-start.3
Sparse Core Ops, SparseCore 0:
  91.1 31.0 reduce-scatter.2
where the time goes:
time: 258 us; the launch traced here: 254 us
  blocking collectives  156 us (60%)
  waiting for transfers between devices  45.8 us (18%)
  local copies, waits for them, and re-layouts  16.3 us (6%)
  between operations  14.1 us (5%)
  matrix products  9.32 us (4%)
  other arithmetic  8.77 us (3%)
  starting transfers between devices  4.11 us (2%)
    unnamed x1, blocking collectives  124 us
    all_to_all x1, blocking collectives, shards(): lax.all_to_all(half_virt, 'orb', split_axis=0, concat_axis=1, tiled=True)  31.4 us
    reduce_scatter x1, waiting for transfers between devices, shards(): lax.psum_scatter(partial_pol, 'aux', scatter_dimension=0, tiled=True)  30 us
    all_to_all x1, waiting for transfers between devices, shards(): lax.all_to_all(both_sides, 'orb', split_axis=1, concat_axis=0, tiled=True)  15.8 us
    mul x1, other arithmetic, shards(): screened = coulomb_blocks * mask[None, :, :]  7.98 us
    dot_general x1, matrix products, shards(): jnp.dot(screened.reshape(naux * mu_rows, nao), green_virt, preferred_elem...  6.62 us
    dynamic_slice x2, local copies, waits for them, and re-layouts, shards(): lax.dynamic_slice_in_dim(screened, lax.axis_index('aux') * sig_cols, sig_...  6.4 us
  transfers between devices with their start and end apart: 2, of which 2 were waited for; matrix products, arithmetic and copies ran while one was open for 3% of the time, Pallas kernels for 0%

commit v1 on v0

v1 whole, which is shorter than its diff:
```python
import jax
import jax.numpy as jnp
from jax import lax
from jax.sharding import PartitionSpec as P

BLK = 8


def gather_virt(green_virt):
    ranks = lax.axis_size("aux")
    me = lax.axis_index("aux")
    own = green_virt.T
    up = [(i, (i + 1) % ranks) for i in range(ranks)]
    down = [(i, (i - 1) % ranks) for i in range(ranks)]
    cols = own.shape[0]
    whole = jnp.zeros((ranks * cols, own.shape[1]), own.dtype)
    whole = lax.dynamic_update_slice_in_dim(whole, own, me * cols, 0)
    from_below, from_above = own, own
    for step in range(1, ranks // 2 + 1):
        from_below = lax.ppermute(from_below, "aux", up)
        whole = lax.dynamic_update_slice_in_dim(whole, from_below, lax.rem(me - step + ranks, ranks) * cols, 0)
        if 2 * step < ranks:
            from_above = lax.ppermute(from_above, "aux", down)
            whole = lax.dynamic_update_slice_in_dim(whole, from_above, lax.rem(me + step, ranks) * cols, 0)
    return whole


def shards(coulomb_blocks, occupancy, green_occ, green_virt):
    naux, mu_rows, nao = coulomb_blocks.shape
    ranks = lax.axis_size("orb")
    share = naux // lax.axis_size("aux")
    mask = jnp.repeat(jnp.repeat(occupancy, BLK, 0), BLK, 1).astype(jnp.bfloat16)
    own = lax.dynamic_slice_in_dim(coulomb_blocks, lax.axis_index("aux") * share, share, 0)
    screened = lax.all_to_all(own * mask[None], "orb", split_axis=0, concat_axis=0, tiled=True)
    screened = screened.reshape(nao, nao)
    virt_t = gather_virt(green_virt)
    half_virt = lax.dot_general(screened, virt_t, (((1,), (1,)), ((), ())), preferred_element_type=jnp.float32)
    both_sides = jnp.dot(green_occ, half_virt.astype(jnp.bfloat16), preferred_element_type=jnp.float32)
    both_sides = both_sides.astype(jnp.bfloat16).reshape(ranks, mu_rows, nao)
    returned = lax.all_to_all(both_sides, "orb", split_axis=0, concat_axis=0, tiled=True)
    partial_pol = jnp.einsum("qls,pls->qp", coulomb_blocks, returned * mask[None], preferred_element_type=jnp.float32)
    parts = lax.all_to_all(partial_pol, "orb", split_axis=0, concat_axis=0, tiled=True)
    return parts.reshape(ranks, naux // ranks, share).sum(0).T


def solution(mesh):
    in_specs = (P(None, "orb", None), P("orb", None), P(), P(None, "aux"))
    out_specs = P("aux", "orb")
    return jax.shard_map(shards, mesh=mesh, in_specs=in_specs, out_specs=out_specs, check_vma=False)
```

time: 258 us -> 91.9 us (0.36); the launches traced: 254 us -> 91.4 us
  blocking collectives: 156 us -> 40.7 us
  waiting for transfers between devices: 45.8 us -> 12.5 us
  starting transfers between devices: 4.11 us -> 19.7 us
  between operations: 14.1 us -> 0.12 us
  local copies, waits for them, and re-layouts: 16.3 us -> 4.02 us
  other arithmetic: 8.77 us -> 4.62 us
    unnamed x1 -> x0, blocking collectives: 124 us -> none
    reduce_scatter x1 -> x0, waiting for transfers between devices: 30 us -> none  [shards(): lax.psum_scatter(partial_pol, 'aux', scatter_dimension=0, tiled=True)]
    all_to_all x1, waiting for transfers between devices: 15.8 us -> 0.01 us  [shards(): lax.all_to_all(own * mask[None], 'orb', split_axis=0, concat_axis=0, tile...]
    ppermute x0 -> x7, waiting for transfers between devices: none -> 12.5 us  [the longest x4 12.5 us: gather_virt(): from_below = lax.ppermute(from_below, 'aux', up)]
    ppermute x0 -> x7, starting transfers between devices: none -> 11.1 us  [the longest x3 9.38 us: gather_virt(): from_above = lax.ppermute(from_above, 'aux', down)]
    all_to_all x1 -> x2, blocking collectives: 31.4 us -> 40.7 us  [the longest x1 29.8 us: shards(): lax.all_to_all(both_sides, 'orb', split_axis=0, concat_axis=0, tiled=True)]
    dynamic_slice x2 -> x0, local copies, waits for them, and re-layouts: 6.4 us -> none  [shards(): lax.dynamic_slice_in_dim(screened, lax.axis_index('aux') * sig_cols, sig_...]
    mul x1 -> x2, other arithmetic: 7.98 us -> 2.49 us  [the longest x1 2.4 us: shards(): own * mask[None]]
  transfers between devices with their start and end apart: 2 -> 8, of which waited for: 2 -> 4; matrix products, arithmetic and copies ran while one was open for 3% -> 3% of each run, Pallas kernels for 0% -> 0%
where the time goes in v1:
time: 91.9 us; the launch traced here: 91.4 us
  blocking collectives  40.7 us (44%)
  starting transfers between devices  19.7 us (21%)
  waiting for transfers between devices  12.5 us (14%)
  matrix products  9.82 us (11%)
  other arithmetic  4.62 us (5%)
  local copies, waits for them, and re-layouts  4.02 us (4%)
    all_to_all x1, blocking collectives, shards(): lax.all_to_all(both_sides, 'orb', split_axis=0, concat_axis=0, tiled=True)  29.8 us
    ppermute x4, waiting for transfers between devices, gather_virt(): from_below = lax.ppermute(from_below, 'aux', up)  12.5 us
    all_to_all x1, blocking collectives, shards(): lax.all_to_all(partial_pol, 'orb', split_axis=0, concat_axis=0, tiled=True)  10.9 us
    ppermute x3, starting transfers between devices, gather_virt(): from_above = lax.ppermute(from_above, 'aux', down)  9.38 us
    all_to_all x1, starting transfers between devices, shards(): lax.all_to_all(own * mask[None], 'orb', split_axis=0, concat_axis=0, tile...  8.59 us
    dot_general x1, matrix products, shards(): jnp.einsum('qls,pls->qp', coulomb_blocks, returned * mask[None], preferre...  6.77 us
    dot_general x1, matrix products, shards(): jnp.dot(green_occ, half_virt.astype(jnp.bfloat16), preferred_element_type...  3.05 us
    mul x1, other arithmetic, shards(): own * mask[None]  2.4 us
  transfers between devices with their start and end apart: 8, of which 4 were waited for; matrix products, arithmetic and copies ran while one was open for 3% of the time, Pallas kernels for 0%

profile of v1, /device:TPU:1, one launch (start us, length us, event | category | flops | bytes accessed | tf_op | source)
XLA Modules:
  0.0 91.4 jit_solution(6283176211767009197)
XLA Ops:
  0.0 0.0 copy-start
  0.0 0.8 convert_element_type.24
  0.8 0.1 copy.12
  0.9 0.1 copy.13
  1.1 0.0 copy-start.1
  1.1 2.4 %dynamic-slice_multiply_fusion = bf16[32,24,768]{2,1,0:T(8,128)(2,1)} fusion(bf16[256,24,768]{2,1,0:T(8,128)(2,1)} %param.4, s32[]{:T(128)S(6)} %select_n.27, bf16[24,768]{1,0:T(8,128)(2,1)S(1)} %copy.13), kind=kLoop, calls=%fused_computation.5 | loop fusion | flops 589824 | bytes 2396164 | tf_op jit(solution)/shard_map/mul | solution.py:34
  3.5 0.0 copy-done.1
  3.5 8.6 %all-to-all-start = ((bf16[32,24,768]{2,1,0:T(8,128)(2,1)}), bf16[32,24,768]{2,1,0:T(8,128)(2,1)S(1)}, u32[]{:S(2)}, u32[]{:S(2)}) async-start(bf16[32,24,768]{2,1,0:T(8,128)(2,1)} %dynamic-slice_multiply_fusion), calls=%async_computation | async-start | bytes 2359296 | tf_op jit(solution)/shard_map/all_to_all | solution.py:34
  12.1 1.7 %collective-permute-start = (bf16[96,768]{1,0:T(8,128)(2,1)}, bf16[96,768]{1,0:T(8,128)(2,1)}, u32[]{:S(2)}, u32[]{:S(2)}) collective-permute-start(bf16[96,768]{1,0:T(8,128)(2,1)} %bitcast.3), channel_id=1, source_target_pairs={{0,1},{1,2},{2,3},{3,4},{4,5},{5,6},{6,7},{7,0},{8,9},{9,10},{10,1... | collective-permute-start | bytes 442376 | tf_op jit(solution)/shard_map/ppermute | solution.py:20
  13.8 4.0 %collective-permute-start.1 = (bf16[96,768]{1,0:T(8,128)(2,1)}, bf16[96,768]{1,0:T(8,128)(2,1)}, u32[]{:S(2)}, u32[]{:S(2)}) collective-permute-start(bf16[96,768]{1,0:T(8,128)(2,1)} %bitcast.3), channel_id=1, source_target_pairs={{0,7},{1,0},{2,1},{3,2},{4,3},{5,4},{6,5},{7,6},{8,15},{9,8},{10,9... | collective-permute-start | bytes 442376 | tf_op jit(solution)/shard_map/ppermute | solution.py:23
  17.8 0.1 broadcast_in_dim.13
  17.9 0.9 %constant_dynamic-update-slice_fusion.7 = bf16[768,768]{1,0:T(8,128)(2,1)S(1)} fusion(bf16[768,768]{1,0:T(8,128)(2,1)S(1)} %broadcast_in_dim.13, s32[]{:T(128)S(6)} %select_n.28, bf16[768,96]{0,1:T(8,128)(2,1)} %param.7), kind=kLoop, calls=%fused_computation.17 | loop fusion | bytes 294916 | tf_op jit(solution)/shard_map/dynamic_update_slice | solution.py:17
  18.8 3.3 %collective-permute-done = bf16[96,768]{1,0:T(8,128)(2,1)} collective-permute-done((bf16[96,768]{1,0:T(8,128)(2,1)}, bf16[96,768]{1,0:T(8,128)(2,1)}, u32[]{:S(2)}, u32[]{:S(2)}) %collective-permute-start) | collective-permute-done | bytes 147488 | tf_op jit(solution)/shard_map/ppermute | solution.py:20
  22.1 0.0 collective-permute-start.2
  22.1 0.0 collective-permute-done.1
  22.1 2.7 %collective-permute-start.3 = (bf16[96,768]{1,0:T(8,128)(2,1)}, bf16[96,768]{1,0:T(8,128)(2,1)S(1)}, u32[]{:S(2)}, u32[]{:S(2)}) collective-permute-start(bf16[96,768]{1,0:T(8,128)(2,1)} %collective-permute-done.1), channel_id=1, source_target_pairs={{0,7},{1,0},{2,1},{3,2},{4,3},{5,4},{6,5},{7,6},{8,15},{9,8},{10,9... | collective-permute-start | bytes 442376 | tf_op jit(solution)/shard_map/ppermute | solution.py:23
  24.8 0.9 %constant_dynamic-update-slice_fusion.6 = bf16[768,768]{1,0:T(8,128)(2,1)S(1)} fusion(bf16[768,768]{1,0:T(8,128)(2,1)S(1)} %constant_dynamic-update-slice_fusion.7, bf16[96,768]{1,0:T(8,128)(2,1)} %collective-permute-done, s32[]{:T(128)S(6)} %select_n.29), kind=kLoop, calls=%fused_computation.16 | loop fusion | bytes 294916 | tf_op jit(solution)/shard_map/dynamic_update_slice | solution.py:21
  25.7 0.9 %constant_dynamic-update-slice_fusion.5 = bf16[768,768]{1,0:T(8,128)(2,1)S(1)} fusion(bf16[768,768]{1,0:T(8,128)(2,1)S(1)} %constant_dynamic-update-slice_fusion.6, bf16[96,768]{1,0:T(8,128)(2,1)} %collective-permute-done.1, s32[]{:T(128)S(6)} %select_n.30), kind=kLoop, calls=%fused_computation.15 | loop fusion | bytes 294916 | tf_op jit(solution)/shard_map/dynamic_update_slice | solution.py:24
  26.6 1.5 %collective-permute-done.2 = bf16[96,768]{1,0:T(8,128)(2,1)S(1)} collective-permute-done((bf16[96,768]{1,0:T(8,128)(2,1)}, bf16[96,768]{1,0:T(8,128)(2,1)S(1)}, u32[]{:S(2)}, u32[]{:S(2)}) %collective-permute-start.2) | collective-permute-done | bytes 147488 | tf_op jit(solution)/shard_map/ppermute | solution.py:20
  28.2 0.0 collective-permute-start.4
  28.2 0.0 collective-permute-done.3
  28.2 2.7 %collective-permute-start.5 = (bf16[96,768]{1,0:T(8,128)(2,1)S(1)}, bf16[96,768]{1,0:T(8,128)(2,1)S(1)}, u32[]{:S(2)}, u32[]{:S(2)}) collective-permute-start(bf16[96,768]{1,0:T(8,128)(2,1)S(1)} %collective-permute-done.3), channel_id=1, source_target_pairs={{0,7},{1,0},{2,1},{3,2},{4,3},{5,4},{6,5},{7,6},{8,15},{9,8},{10,9... | collective-permute-start | bytes 442376 | tf_op jit(solution)/shard_map/ppermute | solution.py:23
  30.9 2.5 %collective-permute-done.4 = bf16[96,768]{1,0:T(8,128)(2,1)S(1)} collective-permute-done((bf16[96,768]{1,0:T(8,128)(2,1)S(1)}, bf16[96,768]{1,0:T(8,128)(2,1)S(1)}, u32[]{:S(2)}, u32[]{:S(2)}) %collective-permute-start.4) | collective-permute-done | bytes 147488 | tf_op jit(solution)/shard_map/ppermute | solution.py:20
  33.4 0.0 collective-permute-start.6
  33.4 0.0 collective-permute-done.5
  33.4 5.1 %collective-permute-done.6 = bf16[96,768]{1,0:T(8,128)(2,1)S(1)} collective-permute-done((bf16[96,768]{1,0:T(8,128)(2,1)S(1)}, bf16[96,768]{1,0:T(8,128)(2,1)S(1)}, u32[]{:S(2)}, u32[]{:S(2)}) %collective-permute-start.6) | collective-permute-done | bytes 147488 | tf_op jit(solution)/shard_map/ppermute | solution.py:20
  38.6 0.0 all-to-all-done
  38.6 0.0 copy-done
  38.6 3.0 %convolution_convert_fusion = bf16[768,768]{0,1:T(8,128)(2,1)} fusion(bf16[768,768]{1,0:T(8,128)(2,1)S(1)} %copy-done, bf16[768,768]{1,0:T(8,128)(2,1)S(1)} %bitcast.19, bf16[768,768]{1,0:T(8,128)(2,1)S(1)} %constant_dynamic-update-slice_fusion), kind=kOutput, calls=%fused_computation.2 | convolution fusion | flops 1813118976 | bytes 4718592 | tf_op jit(solution)/shard_map/dot_general | solution.py:38
  41.7 0.0 copy-start.2
  41.7 29.8 %all_to_all.19 = bf16[32,24,768]{2,1,0:T(8,128)(2,1)S(1)} all-to-all(bf16[32,24,768]{2,1,0:T(8,128)(2,1)} %bitcast.20), channel_id=1, replica_groups=mesh['orb'=32,'aux'=8] {'orb'}, dimensions={0} | all-to-all | bytes 2359296 | tf_op jit(solution)/shard_map/all_to_all | solution.py:40
  71.5 0.0 copy-done.2
  71.5 0.1 broadcast_multiply_fusion
  71.6 6.8 %fusion.3 = f32[256,32]{0,1:T(8,128)S(1)} fusion(bf16[256,24,768]{2,1,0:T(8,128)(2,1)} %param.4, bf16[32,24,768]{2,1,0:T(8,128)(2,1)S(1)} %broadcast_multiply_fusion), kind=kOutput, calls=%fused_computation.6 | convolution fusion | flops 301989888 | bytes 10649600 | tf_op jit(solution)/shard_map/qls,pls->qp/dot_general | solution.py:41
  78.3 0.1 copy.16
  78.4 0.1 reshape.22
  78.6 10.9 %all_to_all.20 = f32[32,1,256]{2,1,0:T(1,128)S(1)} all-to-all(f32[32,1,256]{2,1,0:T(1,128)S(1)} %reshape.22), channel_id=1, replica_groups=mesh['orb'=32,'aux'=8] {'orb'}, dimensions={0} | all-to-all | bytes 65536 | tf_op jit(solution)/shard_map/all_to_all | solution.py:42
  89.4 0.5 broadcast.9
  90.0 0.7 reduce.1
  90.7 0.1 reshape.23
  90.8 0.6 reduce_sum.9
  (7 shorter events, 0.1 us)
Async XLA Ops:
  0.0 38.6 %copy-start = (bf16[768,768]{1,0:T(8,128)(2,1)S(1)}, bf16[768,768]{1,0:T(8,128)(2,1)}, u32[]{:S(2)}) copy-start(bf16[768,768]{1,0:T(8,128)(2,1)} %param.6) | copy-start | bytes 3538948
  1.1 2.4 %copy-start.1 = (bf16[24,768]{1,0:T(8,128)(2,1)}, bf16[24,768]{1,0:T(8,128)(2,1)S(1)}, u32[]{:S(2)}) copy-start(bf16[24,768]{1,0:T(8,128)(2,1)S(1)} %copy.13) | copy-start | bytes 110596
  3.5 35.2 %all-to-all-start = ((bf16[32,24,768]{2,1,0:T(8,128)(2,1)}), bf16[32,24,768]{2,1,0:T(8,128)(2,1)S(1)}, u32[]{:S(2)}, u32[]{:S(2)}) async-start(bf16[32,24,768]{2,1,0:T(8,128)(2,1)} %dynamic-slice_multiply_fusion), calls=%async_computation | async-start | bytes 2359296 | tf_op jit(solution)/shard_map/all_to_all | solution.py:34
  12.1 10.0 %collective-permute-start = (bf16[96,768]{1,0:T(8,128)(2,1)}, bf16[96,768]{1,0:T(8,128)(2,1)}, u32[]{:S(2)}, u32[]{:S(2)}) collective-permute-start(bf16[96,768]{1,0:T(8,128)(2,1)} %bitcast.3), channel_id=1, source_target_pairs={{0,1},{1,2},{2,3},{3,4},{4,5},{5,6},{6,7},{7,0},{8,9},{9,10},{10,1... | collective-permute-start | bytes 442376 | tf_op jit(solution)/shard_map/ppermute | solution.py:20
  13.8 8.3 %collective-permute-start.1 = (bf16[96,768]{1,0:T(8,128)(2,1)}, bf16[96,768]{1,0:T(8,128)(2,1)}, u32[]{:S(2)}, u32[]{:S(2)}) collective-permute-start(bf16[96,768]{1,0:T(8,128)(2,1)} %bitcast.3), channel_id=1, source_target_pairs={{0,7},{1,0},{2,1},{3,2},{4,3},{5,4},{6,5},{7,6},{8,15},{9,8},{10,9... | collective-permute-start | bytes 442376 | tf_op jit(solution)/shard_map/ppermute | solution.py:23
  22.1 6.1 %collective-permute-start.2 = (bf16[96,768]{1,0:T(8,128)(2,1)}, bf16[96,768]{1,0:T(8,128)(2,1)S(1)}, u32[]{:S(2)}, u32[]{:S(2)}) collective-permute-start(bf16[96,768]{1,0:T(8,128)(2,1)} %collective-permute-done), channel_id=1, source_target_pairs={{0,1},{1,2},{2,3},{3,4},{4,5},{5,6},{6,7},{7,0},{8,9},{9,10},{10,1... | collective-permute-start | bytes 442376 | tf_op jit(solution)/shard_map/ppermute | solution.py:20
  22.1 6.1 %collective-permute-start.3 = (bf16[96,768]{1,0:T(8,128)(2,1)}, bf16[96,768]{1,0:T(8,128)(2,1)S(1)}, u32[]{:S(2)}, u32[]{:S(2)}) collective-permute-start(bf16[96,768]{1,0:T(8,128)(2,1)} %collective-permute-done.1), channel_id=1, source_target_pairs={{0,7},{1,0},{2,1},{3,2},{4,3},{5,4},{6,5},{7,6},{8,15},{9,8},{10,9... | collective-permute-start | bytes 442376 | tf_op jit(solution)/shard_map/ppermute | solution.py:23
  28.2 5.2 %collective-permute-start.4 = (bf16[96,768]{1,0:T(8,128)(2,1)S(1)}, bf16[96,768]{1,0:T(8,128)(2,1)S(1)}, u32[]{:S(2)}, u32[]{:S(2)}) collective-permute-start(bf16[96,768]{1,0:T(8,128)(2,1)S(1)} %collective-permute-done.2), channel_id=1, source_target_pairs={{0,1},{1,2},{2,3},{3,4},{4,5},{5,6},{6,7},{7,0},{8,9},{9,10},{10,1... | collective-permute-start | bytes 442376 | tf_op jit(solution)/shard_map/ppermute | solution.py:20
  28.2 5.2 %collective-permute-start.5 = (bf16[96,768]{1,0:T(8,128)(2,1)S(1)}, bf16[96,768]{1,0:T(8,128)(2,1)S(1)}, u32[]{:S(2)}, u32[]{:S(2)}) collective-permute-start(bf16[96,768]{1,0:T(8,128)(2,1)S(1)} %collective-permute-done.3), channel_id=1, source_target_pairs={{0,7},{1,0},{2,1},{3,2},{4,3},{5,4},{6,5},{7,6},{8,15},{9,8},{10,9... | collective-permute-start | bytes 442376 | tf_op jit(solution)/shard_map/ppermute | solution.py:23
  33.4 5.2 %collective-permute-start.6 = (bf16[96,768]{1,0:T(8,128)(2,1)S(1)}, bf16[96,768]{1,0:T(8,128)(2,1)S(1)}, u32[]{:S(2)}, u32[]{:S(2)}) collective-permute-start(bf16[96,768]{1,0:T(8,128)(2,1)S(1)} %collective-permute-done.4), channel_id=1, source_target_pairs={{0,1},{1,2},{2,3},{3,4},{4,5},{5,6},{6,7},{7,0},{8,9},{9,10},{10,1... | collective-permute-start | bytes 442376 | tf_op jit(solution)/shard_map/ppermute | solution.py:20
  41.7 29.8 %copy-start.2 = (bf16[24,768]{1,0:T(8,128)(2,1)S(1)}, bf16[24,768]{1,0:T(8,128)(2,1)}, u32[]{:S(2)}) copy-start(bf16[24,768]{1,0:T(8,128)(2,1)} %copy-done.1) | copy-start | bytes 110596

commit v2 on v0

v2 whole, which is shorter than its diff:
```python
import functools

import jax
import jax.numpy as jnp
from jax import lax
from jax.experimental import pallas as pl
from jax.experimental.pallas import tpu as pltpu
from jax.sharding import PartitionSpec as P

BLK = 8
LANES = 128
SCREEN_FLOPS = 1000
ALL_VMEM = 60 * 1024 * 1024
MOST_VMEM = 57 * 1024 * 1024
WIDE_VMEM = 10 * 1024 * 1024
PART = 64
SMALL_VMEM = 4 * 1024 * 1024
VMEM = pl.BlockSpec(memory_space=pltpu.VMEM)


def expand(occupancy, rows, cols):
    blocks = occupancy.shape[1]
    block = lax.broadcasted_iota(jnp.int32, (blocks, cols), 0)
    col = lax.broadcasted_iota(jnp.int32, (blocks, cols), 1)
    spread = (lax.div(col, BLK) == block).astype(jnp.float32)
    wide = jnp.dot(occupancy.astype(jnp.float32), spread, preferred_element_type=jnp.float32)
    return jnp.concatenate([jnp.broadcast_to(wide[i : i + 1], (BLK, cols)) for i in range(rows // BLK)], axis=0)


def screen_kernel(coulomb_ref, occupancy_ref, out_ref):
    rows, cols = coulomb_ref.shape[1:]
    mask = expand(occupancy_ref[...], rows, cols).astype(coulomb_ref.dtype)
    out_ref[...] = coulomb_ref[...] * mask[None]


def screen(coulomb_blocks, occupancy, share):
    rows, cols = coulomb_blocks.shape[1:]
    return pl.pallas_call(
        screen_kernel,
        grid=(1,),
        in_specs=[
            pl.BlockSpec((share, rows, cols), lambda i: (lax.axis_index("aux"), 0, 0)),
            pl.BlockSpec(occupancy.shape, lambda i: (0, 0)),
        ],
        out_specs=pl.BlockSpec((share, rows, cols), lambda i: (0, 0, 0)),
        out_shape=jax.ShapeDtypeStruct((share, rows, cols), coulomb_blocks.dtype),
        compiler_params=pltpu.CompilerParams(vmem_limit_bytes=ALL_VMEM),
        cost_estimate=pl.CostEstimate(flops=SCREEN_FLOPS, bytes_accessed=0, transcendentals=0),
        name="screen",
    )(coulomb_blocks, occupancy)


def fetch_virt(green_virt):
    ranks = lax.axis_size("aux")
    orbs = lax.axis_size("orb")
    own = green_virt.T
    half = own.shape[0] // 2
    own_half = lax.dynamic_slice_in_dim(own, lax.rem(lax.axis_index("orb"), 2) * half, half, 0)
    got = []
    for dist in range(1, ranks // 2 + 1):
        pairs = []
        for orb in range(orbs):
            for aux in range(ranks):
                target = (aux - dist if orb % 2 == 0 else aux + dist) % ranks
                pairs.append((orb * ranks + aux, orb * ranks + target))
        got.append(lax.ppermute(own if 2 * dist < ranks else own_half, ("orb", "aux"), pairs))
    return own, got


def swap_cores(blocks):
    pairs = [(i, i ^ 1) for i in range(lax.axis_size("orb"))]
    return [lax.ppermute(block, "orb", pairs) for block in blocks]


def assemble_kernel(ranks, own_ref, *refs):
    (*block_refs, out_ref) = refs
    me, side = lax.axis_index("aux"), lax.rem(lax.axis_index("orb"), 2)
    cols = own_ref.shape[0]
    far = ranks // 2
    out_ref[pl.ds(pl.multiple_of(me * cols, cols), cols), :] = own_ref[...]
    for which in range(2):
        core = side if which == 0 else 1 - side
        for dist in range(1, far + 1):
            ref = block_refs[which * far + dist - 1]
            source = lax.rem(me + ranks + jnp.where(core == 0, dist, -dist), ranks)
            first = source * cols + (core * (cols // 2) if 2 * dist == ranks else 0)
            out_ref[pl.ds(pl.multiple_of(first, cols // 2), ref.shape[0]), :] = ref[...]


def assemble(own, got, other):
    ranks = lax.axis_size("aux")
    blocks = [*got, *other]
    return pl.pallas_call(
        functools.partial(assemble_kernel, ranks),
        in_specs=[VMEM] * (1 + len(blocks)),
        out_specs=VMEM,
        out_shape=jax.ShapeDtypeStruct((ranks * own.shape[0], own.shape[1]), own.dtype),
        compiler_params=pltpu.CompilerParams(vmem_limit_bytes=SMALL_VMEM),
        name="assemble",
    )(own, *blocks)


def apply_virt_kernel(coulomb_ref, virt_ref, occupancy_ref, out_ref, mask):
    rows, count, cols = out_ref.shape

    @pl.when(pl.program_id(0) == 0)
    def _():
        once = expand(occupancy_ref[...], rows, cols)
        mask[...] = jnp.concatenate([once, once], axis=0).astype(mask.dtype)

    @pl.loop(0, count // PART)
    def _(i):
        here = pl.ds(pl.multiple_of(i * PART * rows, PART * rows), PART * rows)
        screened = coulomb_ref[here, :].reshape(PART // 2, 2 * rows, cols) * mask[...][None]
        half = jnp.dot(screened.reshape(PART * rows, cols), virt_ref[...], preferred_element_type=jnp.float32)
        half = half.reshape(PART, rows, cols).astype(out_ref.dtype)
        out_ref[:, pl.ds(pl.multiple_of(i * PART, PART), PART), :] = jnp.swapaxes(half, 0, 1)


def apply_virt(coulomb_blocks, virt_t, occupancy, count=64):
    naux, rows, cols = coulomb_blocks.shape
    dtype = coulomb_blocks.dtype
    return pl.pallas_call(
        apply_virt_kernel,
        grid=(naux // count,),
        in_specs=[
            pl.BlockSpec((count * rows, cols), lambda i: (i, 0)),
            pl.BlockSpec(virt_t.shape, lambda i: (0, 0)),
            pl.BlockSpec(occupancy.shape, lambda i: (0, 0)),
        ],
        out_specs=pl.BlockSpec((rows, count, cols), lambda i: (0, i, 0)),
        out_shape=jax.ShapeDtypeStruct((rows, naux, cols), dtype),
        scratch_shapes=[pltpu.VMEM((2 * rows, cols), dtype)],
        compiler_params=pltpu.CompilerParams(vmem_limit_bytes=ALL_VMEM),
        name="apply_virt",
    )(coulomb_blocks.reshape(naux * rows, cols), virt_t, occupancy)


def apply_occ_kernel(occ_ref, screened_ref, out_ref):
    out_ref[...] = jnp.dot(occ_ref[...], screened_ref[...], preferred_element_type=jnp.float32).astype(out_ref.dtype)


def apply_occ(green_occ, screened):
    return pl.pallas_call(
        apply_occ_kernel,
        in_specs=[VMEM] * 2,
        out_specs=VMEM,
        out_shape=jax.ShapeDtypeStruct(screened.shape, screened.dtype),
        compiler_params=pltpu.CompilerParams(vmem_limit_bytes=WIDE_VMEM),
        name="apply_occ",
    )(green_occ, screened)


def contract_kernel(returned_ref, half_ref, out_ref, left, right, sem):
    rows, naux, cols = left.shape
    share = right.shape[1]
    chunks = sem.shape[0]
    depth = rows // chunks

    def fetch(i):
        here = pl.ds(i * depth, depth)
        return pltpu.make_async_copy(half_ref.at[here], left.at[here], sem.at[i])

    for i in range(chunks):
        fetch(i).start()

    @pl.loop(0, share // 16)
    def _(i):
        here = pl.ds(pl.multiple_of(i * 16, 16), 16)
        right[:, here, :] = jnp.swapaxes(returned_ref[here], 0, 1)

    out_ref[...] = jnp.zeros(out_ref.shape, out_ref.dtype)

    @pl.loop(0, chunks)
    def _(i):
        fetch(i).wait()
        total = jnp.zeros((naux, share), jnp.float32)
        for j in range(depth):
            total += lax.dot_general(
                left[i * depth + j], right[i * depth + j], (((1,), (1,)), ((), ())), preferred_element_type=jnp.float32
            )
        out_ref[:, :share] += total


def contract(half_rows, returned, chunks=4):
    rows, naux, cols = half_rows.shape
    share = returned.shape[0]
    dtype = half_rows.dtype
    return pl.pallas_call(
        contract_kernel,
        in_specs=[VMEM, pl.BlockSpec(memory_space=pl.ANY)],
        out_specs=VMEM,
        out_shape=jax.ShapeDtypeStruct((naux, LANES), jnp.float32),
        scratch_shapes=[
            pltpu.VMEM((rows, naux, cols), dtype),
            pltpu.VMEM((rows, share, cols), dtype),
            pltpu.SemaphoreType.DMA((chunks,)),
        ],
        compiler_params=pltpu.CompilerParams(vmem_limit_bytes=MOST_VMEM),
        name="contract",
    )(returned, half_rows)


def finish_kernel(parts_ref, out_ref):
    out_ref[...] = jnp.sum(parts_ref[...], axis=0)[:, : out_ref.shape[1]]


def finish(parts, share):
    return pl.pallas_call(
        finish_kernel,
        in_specs=[VMEM],
        out_specs=pl.BlockSpec((parts.shape[1], share), lambda: (0, 0)),
        out_shape=jax.ShapeDtypeStruct((parts.shape[1], share), parts.dtype),
        name="finish",
    )(parts)


def shards(coulomb_blocks, occupancy, green_occ, green_virt):
    naux, mu_rows, nao = coulomb_blocks.shape
    ranks = lax.axis_size("orb")
    planes = lax.axis_size("aux")
    share = naux // planes
    own = screen(coulomb_blocks, occupancy, share)
    own_virt, got = fetch_virt(green_virt)
    screened = lax.all_to_all(own, "orb", split_axis=0, concat_axis=0, tiled=True).reshape(nao, nao)
    half_occ = apply_occ(green_occ, screened)
    half_occ, *got = lax.optimization_barrier((half_occ, *got))
    virt_t = assemble(own_virt, got, swap_cores(got))
    half_rows = apply_virt(coulomb_blocks, virt_t, occupancy)
    returned = lax.all_to_all(half_occ.reshape(ranks, mu_rows, nao), "orb", split_axis=0, concat_axis=0, tiled=True)
    partial_pol = contract(half_rows, returned)
    parts = partial_pol.reshape(ranks, naux // ranks, LANES)
    parts = lax.all_to_all(parts, "orb", split_axis=0, concat_axis=0, tiled=True)
    return finish(parts, share).T


def solution(mesh):
    in_specs = (P(None, "orb", None), P("orb", None), P(), P(None, "aux"))
    out_specs = P("aux", "orb")
    return jax.shard_map(shards, mesh=mesh, in_specs=in_specs, out_specs=out_specs, check_vma=False)
```

time: 258 us -> 80.9 us (0.31); the launches traced: 254 us -> 80.4 us
  blocking collectives: 156 us -> 13.6 us
  waiting for transfers between devices: 45.8 us -> 12.9 us
  Pallas kernels: 0 us -> 25.8 us
  starting transfers between devices: 4.11 us -> 26 us
  local copies, waits for them, and re-layouts: 16.3 us -> 2.06 us
  between operations: 14.1 us -> 0.07 us
  matrix products: 9.32 us -> 0 us
  other arithmetic: 8.77 us -> 0 us
    unnamed x1 -> x0, blocking collectives: 124 us -> none
    reduce_scatter x1 -> x0, waiting for transfers between devices: 30 us -> none  [shards(): lax.psum_scatter(partial_pol, 'aux', scatter_dimension=0, tiled=True)]
    pallas_call x0 -> x6, Pallas kernels: none -> 25.8 us  [the longest x1 12.9 us: apply_virt(): pl.pallas_call(apply_virt_kernel, grid=(naux // count,), in_specs=[pl.Blo...]
    all_to_all x1, blocking collectives: 31.4 us -> 13.6 us  [shards(): lax.all_to_all(parts, 'orb', split_axis=0, concat_axis=0, tiled=True)]
    all_to_all x1 -> x2, starting transfers between devices: 4.07 us -> 15.9 us  [the longest x1 8.72 us: shards(): lax.all_to_all(own, 'orb', split_axis=0, concat_axis=0, tiled=True)]
    ppermute x0 -> x8, starting transfers between devices: none -> 10.1 us  [the longest x4 9.01 us: fetch_virt(): lax.ppermute(own if 2 * dist < ranks else own_half, ('orb', 'aux'), pairs)]
    dot_general x3 -> x0, matrix products: 9.32 us -> none  [the longest x1 6.62 us: shards(): jnp.dot(screened.reshape(naux * mu_rows, nao), green_virt, preferred_elem...]
    mul x1 -> x0, other arithmetic: 7.98 us -> none  [shards(): screened = coulomb_blocks * mask[None, :, :]]
  transfers between devices with their start and end apart: 2 -> 10, of which waited for: 2 -> 4; matrix products, arithmetic and copies ran while one was open for 3% -> 0% of each run, Pallas kernels for 0% -> 19%
where the time goes in v2:
time: 80.9 us; the launch traced here: 80.4 us
  starting transfers between devices  26 us (32%)
  Pallas kernels  25.8 us (32%)
  blocking collectives  13.6 us (17%)
  waiting for transfers between devices  12.9 us (16%)
  local copies, waits for them, and re-layouts  2.06 us (3%)
    all_to_all x1, blocking collectives, shards(): lax.all_to_all(parts, 'orb', split_axis=0, concat_axis=0, tiled=True)  13.6 us
    pallas_call x1, Pallas kernels, apply_virt(): pl.pallas_call(apply_virt_kernel, grid=(naux // count,), in_specs=[pl.Blo...  12.9 us
    ppermute x4, starting transfers between devices, fetch_virt(): lax.ppermute(own if 2 * dist < ranks else own_half, ('orb', 'aux'), pairs)  9.01 us
    all_to_all x1, waiting for transfers between devices, shards(): lax.all_to_all(own, 'orb', split_axis=0, concat_axis=0, tiled=True)  8.96 us
    all_to_all x1, starting transfers between devices, shards(): lax.all_to_all(own, 'orb', split_axis=0, concat_axis=0, tiled=True)  8.72 us
    all_to_all x1, starting transfers between devices, shards(): lax.all_to_all(half_occ.reshape(ranks, mu_rows, nao), 'orb', split_axis=0...  7.14 us
    pallas_call x1, Pallas kernels, contract(): pl.pallas_call(contract_kernel, in_specs=[VMEM, pl.BlockSpec(memory_space...  6.62 us
    pallas_call x1, Pallas kernels, screen(): pl.pallas_call(screen_kernel, grid=(1,), in_specs=[pl.BlockSpec((share, r...  2.52 us
  transfers between devices with their start and end apart: 10, of which 4 were waited for; matrix products, arithmetic and copies ran while one was open for 0% of the time, Pallas kernels for 19%

profile of v2, /device:TPU:1, one launch (start us, length us, event | category | flops | bytes accessed | tf_op | source)
XLA Modules:
  0.0 80.4 jit_solution(18299080014352030859)
XLA Ops:
  0.0 2.5 %screen.1 = bf16[32,24,768]{2,1,0:T(8,128)(2,1)} custom-call(bf16[256,24,768]{2,1,0:T(8,128)(2,1)} %coulomb_ref.1, s32[3,96]{1,0:T(4,128)} %occupancy_ref.3), custom_call_target="tpu_custom_call" | custom-call | flops 1000 | tf_op jit(solution)/shard_map/screen/pallas_call | solution.py:38
  2.5 0.0 copy-start.2
  2.5 0.0 copy-start.1
  2.5 8.7 %all-to-all-start = ((bf16[32,24,768]{2,1,0:T(8,128)(2,1)}), bf16[32,24,768]{2,1,0:T(8,128)(2,1)S(1)}, u32[]{:S(2)}, u32[]{:S(2)}) async-start(bf16[32,24,768]{2,1,0:T(8,128)(2,1)} %screen.1), calls=%async_computation | async-start | bytes 2359296 | tf_op jit(solution)/shard_map/all_to_all | solution.py:225
  11.3 0.0 copy-done.2
  11.3 4.4 %collective-permute-start.2 = (bf16[96,768]{1,0:T(8,128)(2,1)S(1)}, bf16[96,768]{1,0:T(8,128)(2,1)S(1)}, u32[]{:S(2)}, u32[]{:S(2)}) collective-permute-start(bf16[96,768]{1,0:T(8,128)(2,1)S(1)} %bitcast.9), channel_id=1, source_target_pairs={{0,5},{1,6},{2,7},{3,0},{4,1},{5,2},{6,3},{7,4},{8,11},{9,12},{10,... | collective-permute-start | bytes 442376 | tf_op jit(solution)/shard_map/ppermute | solution.py:66
  15.7 3.3 %collective-permute-start.1 = (bf16[96,768]{1,0:T(8,128)(2,1)S(1)}, bf16[96,768]{1,0:T(8,128)(2,1)S(1)}, u32[]{:S(2)}, u32[]{:S(2)}) collective-permute-start(bf16[96,768]{1,0:T(8,128)(2,1)S(1)} %bitcast.10), channel_id=1, source_target_pairs={{0,6},{1,7},{2,0},{3,1},{4,2},{5,3},{6,4},{7,5},{8,10},{9,11},{10,... | collective-permute-start | bytes 442376 | tf_op jit(solution)/shard_map/ppermute | solution.py:66
  19.0 0.7 collective-permute-start
  19.7 0.5 collective-permute-start.3
  20.3 9.0 %all-to-all-done = bf16[32,24,768]{2,1,0:T(8,128)(2,1)S(1)} async-done(((bf16[32,24,768]{2,1,0:T(8,128)(2,1)}), bf16[32,24,768]{2,1,0:T(8,128)(2,1)S(1)}, u32[]{:S(2)}, u32[]{:S(2)}) %all-to-all-start) | async-done | bytes 1179680 | tf_op jit(solution)/shard_map/all_to_all | solution.py:225
  29.2 0.0 copy-done.1
  29.2 2.1 %apply_occ.1 = bf16[768,768]{1,0:T(8,128)(2,1)} custom-call(bf16[768,768]{1,0:T(8,128)(2,1)S(1)} %copy-done.1, bf16[768,768]{1,0:T(8,128)(2,1)S(1)} %bitcast.8), custom_call_target="tpu_custom_call" | custom-call | tf_op jit(solution)/shard_map/apply_occ/pallas_call | solution.py:144
  31.4 1.4 %collective-permute-done.3.refs_3_ = bf16[48,768]{1,0:T(8,128)(2,1)S(1)} collective-permute-done((bf16[48,768]{1,0:T(8,128)(2,1)S(1)}, bf16[48,768]{1,0:T(8,128)(2,1)S(1)}, u32[]{:S(2)}, u32[]{:S(2)}) %collective-permute-start.3) | collective-permute-done | bytes 73760 | tf_op jit(solution)/shard_map/ppermute | solution.py:66
  32.7 0.0 collective-permute-done.2.refs_2_
  32.7 0.0 collective-permute-done.1.refs_1_
  32.7 0.0 collective-permute-done.refs_0_
  32.8 7.1 %all-to-all-start.1 = ((bf16[32,24,768]{2,1,0:T(8,128)(2,1)}), bf16[32,24,768]{2,1,0:T(8,128)(2,1)S(1)}, u32[]{:S(2)}, u32[]{:S(2)}) async-start(bf16[32,24,768]{2,1,0:T(8,128)(2,1)} %bitcast.3), calls=%async_computation.1 | async-start | bytes 2359296 | tf_op jit(solution)/shard_map/all_to_all | solution.py:230
  39.9 0.3 collective-permute-start.4
  40.2 0.3 collective-permute-start.5
  40.5 0.2 collective-permute-start.6
  40.7 0.3 collective-permute-start.7
  41.0 1.0 %collective-permute-done.7.refs_7_ = bf16[48,768]{1,0:T(8,128)(2,1)S(1)} collective-permute-done((bf16[48,768]{1,0:T(8,128)(2,1)S(1)}, bf16[48,768]{1,0:T(8,128)(2,1)S(1)}, u32[]{:S(2)}, u32[]{:S(2)}) %collective-permute-start.7) | collective-permute-done | bytes 73760 | tf_op jit(solution)/shard_map/ppermute | solution.py:72
  42.0 0.0 collective-permute-done.4.refs_4_
  42.0 0.0 collective-permute-done.5.refs_5_
  42.0 0.0 collective-permute-done.6.refs_6_
  42.0 0.1 assemble.1.virt_ref
  42.1 0.0 copy-start
  42.1 1.0 %copy-done = bf16[768,768]{1,0:T(8,128)(2,1)} copy-done((bf16[768,768]{1,0:T(8,128)(2,1)}, bf16[768,768]{1,0:T(8,128)(2,1)S(1)}, u32[]{:S(2)}) %copy-start) | copy-done | bytes 1179672
  43.1 12.9 %apply_virt.1.half_ref = bf16[24,256,768]{2,1,0:T(8,128)(2,1)} custom-call(bf16[6144,768]{1,0:T(8,128)(2,1)} %bitcast.13, bf16[768,768]{1,0:T(8,128)(2,1)} %copy-done, s32[3,96]{1,0:T(4,128)} %occupancy_ref.3), custom_call_target="tpu_custom_call" | custom-call | tf_op jit(solution)/shard_map/apply_virt/pallas_call | solution.py:123
  56.1 1.5 %all-to-all-done.1.returned_ref = bf16[32,24,768]{2,1,0:T(8,128)(2,1)S(1)} async-done(((bf16[32,24,768]{2,1,0:T(8,128)(2,1)}), bf16[32,24,768]{2,1,0:T(8,128)(2,1)S(1)}, u32[]{:S(2)}, u32[]{:S(2)}) %all-to-all-start.1) | async-done | bytes 1179680 | tf_op jit(solution)/shard_map/all_to_all | solution.py:230
  57.6 0.0 copy-start.3
  57.6 1.0 %copy-done.3 = bf16[32,24,768]{2,1,0:T(8,128)(2,1)} copy-done((bf16[32,24,768]{2,1,0:T(8,128)(2,1)}, bf16[32,24,768]{2,1,0:T(8,128)(2,1)S(1)}, u32[]{:S(2)}) %copy-start.3) | copy-done | bytes 1179672
  58.6 6.6 %contract.1 = f32[256,128]{1,0:T(8,128)} custom-call(bf16[32,24,768]{2,1,0:T(8,128)(2,1)} %copy-done.3, bf16[24,256,768]{2,1,0:T(8,128)(2,1)} %apply_virt.1.half_ref), custom_call_target="tpu_custom_call" | custom-call | tf_op jit(solution)/shard_map/contract/pallas_call | solution.py:189
  65.3 13.6 %all_to_all.15.parts_ref = f32[32,8,128]{2,1,0:T(8,128)} all-to-all(f32[32,8,128]{2,1,0:T(8,128)} %bitcast.14), channel_id=1, replica_groups=mesh['orb'=32,'aux'=8] {'orb'}, dimensions={0} | all-to-all | bytes 262144 | tf_op jit(solution)/shard_map/all_to_all | solution.py:233
  78.9 1.5 %finish.1 = f32[8,32]{1,0:T(8,128)} custom-call(f32[32,8,128]{2,1,0:T(8,128)} %all_to_all.15.parts_ref), custom_call_target="tpu_custom_call" | custom-call | tf_op jit(solution)/shard_map/finish/pallas_call | solution.py:209
  (1 shorter events, 0.0 us)
Async XLA Ops:
  2.5 8.7 %copy-start.2 = (bf16[768,96]{0,1:T(8,128)(2,1)S(1)}, bf16[768,96]{0,1:T(8,128)(2,1)}, u32[]{:S(2)}) copy-start(bf16[768,96]{0,1:T(8,128)(2,1)} %param.7) | copy-start | bytes 442372
  2.5 26.7 %copy-start.1 = (bf16[768,768]{1,0:T(8,128)(2,1)S(1)}, bf16[768,768]{1,0:T(8,128)(2,1)}, u32[]{:S(2)}) copy-start(bf16[768,768]{1,0:T(8,128)(2,1)} %occ_ref.1) | copy-start | bytes 3538948
  2.5 26.7 %all-to-all-start = ((bf16[32,24,768]{2,1,0:T(8,128)(2,1)}), bf16[32,24,768]{2,1,0:T(8,128)(2,1)S(1)}, u32[]{:S(2)}, u32[]{:S(2)}) async-start(bf16[32,24,768]{2,1,0:T(8,128)(2,1)} %screen.1), calls=%async_computation | async-start | bytes 2359296 | tf_op jit(solution)/shard_map/all_to_all | solution.py:225
  11.3 21.5 %collective-permute-start.2 = (bf16[96,768]{1,0:T(8,128)(2,1)S(1)}, bf16[96,768]{1,0:T(8,128)(2,1)S(1)}, u32[]{:S(2)}, u32[]{:S(2)}) collective-permute-start(bf16[96,768]{1,0:T(8,128)(2,1)S(1)} %bitcast.9), channel_id=1, source_target_pairs={{0,5},{1,6},{2,7},{3,0},{4,1},{5,2},{6,3},{7,4},{8,11},{9,12},{10,... | collective-permute-start | bytes 442376 | tf_op jit(solution)/shard_map/ppermute | solution.py:66
  15.7 17.1 %collective-permute-start.1 = (bf16[96,768]{1,0:T(8,128)(2,1)S(1)}, bf16[96,768]{1,0:T(8,128)(2,1)S(1)}, u32[]{:S(2)}, u32[]{:S(2)}) collective-permute-start(bf16[96,768]{1,0:T(8,128)(2,1)S(1)} %bitcast.10), channel_id=1, source_target_pairs={{0,6},{1,7},{2,0},{3,1},{4,2},{5,3},{6,4},{7,5},{8,10},{9,11},{10,... | collective-permute-start | bytes 442376 | tf_op jit(solution)/shard_map/ppermute | solution.py:66
  19.0 13.8 %collective-permute-start = (bf16[96,768]{1,0:T(8,128)(2,1)S(1)}, bf16[96,768]{1,0:T(8,128)(2,1)S(1)}, u32[]{:S(2)}, u32[]{:S(2)}) collective-permute-start(bf16[96,768]{1,0:T(8,128)(2,1)S(1)} %bitcast.11), channel_id=1, source_target_pairs={{0,7},{1,0},{2,1},{3,2},{4,3},{5,4},{6,5},{7,6},{8,9},{9,10},{10,1... | collective-permute-start | bytes 442376 | tf_op jit(solution)/shard_map/ppermute | solution.py:66
  19.7 13.0 %collective-permute-start.3 = (bf16[48,768]{1,0:T(8,128)(2,1)S(1)}, bf16[48,768]{1,0:T(8,128)(2,1)S(1)}, u32[]{:S(2)}, u32[]{:S(2)}) collective-permute-start(bf16[48,768]{1,0:T(8,128)(2,1)S(1)} %dynamic-slice_bitcast_fusion), channel_id=1, source_target_pairs={{0,4},{1,5},{2,6},{3,7},{4,0},{5,1},{6,2},{7,3},{8,12},{9,13},{10,... | collective-permute-start | bytes 221192 | tf_op jit(solution)/shard_map/ppermute | solution.py:66
  32.8 24.8 %all-to-all-start.1 = ((bf16[32,24,768]{2,1,0:T(8,128)(2,1)}), bf16[32,24,768]{2,1,0:T(8,128)(2,1)S(1)}, u32[]{:S(2)}, u32[]{:S(2)}) async-start(bf16[32,24,768]{2,1,0:T(8,128)(2,1)} %bitcast.3), calls=%async_computation.1 | async-start | bytes 2359296 | tf_op jit(solution)/shard_map/all_to_all | solution.py:230
  39.9 2.1 %collective-permute-start.4 = (bf16[96,768]{1,0:T(8,128)(2,1)S(1)}, bf16[96,768]{1,0:T(8,128)(2,1)S(1)}, u32[]{:S(2)}, u32[]{:S(2)}) collective-permute-start(bf16[96,768]{1,0:T(8,128)(2,1)S(1)} %collective-permute-done.refs_0_), channel_id=1, source_target_pairs={{0,8},{8,0},{16,24},{24,16},{32,40},{40,32},{48,56},{56,48},{64,72... | collective-permute-start | bytes 442376 | tf_op jit(solution)/shard_map/ppermute | solution.py:72
  40.2 1.8 %collective-permute-start.5 = (bf16[96,768]{1,0:T(8,128)(2,1)S(1)}, bf16[96,768]{1,0:T(8,128)(2,1)S(1)}, u32[]{:S(2)}, u32[]{:S(2)}) collective-permute-start(bf16[96,768]{1,0:T(8,128)(2,1)S(1)} %collective-permute-done.1.refs_1_), channel_id=1, source_target_pairs={{0,8},{8,0},{16,24},{24,16},{32,40},{40,32},{48,56},{56,48},{64,72... | collective-permute-start | bytes 442376 | tf_op jit(solution)/shard_map/ppermute | solution.py:72
  40.5 1.5 %collective-permute-start.6 = (bf16[96,768]{1,0:T(8,128)(2,1)S(1)}, bf16[96,768]{1,0:T(8,128)(2,1)S(1)}, u32[]{:S(2)}, u32[]{:S(2)}) collective-permute-start(bf16[96,768]{1,0:T(8,128)(2,1)S(1)} %collective-permute-done.2.refs_2_), channel_id=1, source_target_pairs={{0,8},{8,0},{16,24},{24,16},{32,40},{40,32},{48,56},{56,48},{64,72... | collective-permute-start | bytes 442376 | tf_op jit(solution)/shard_map/ppermute | solution.py:72
  40.7 1.3 %collective-permute-start.7 = (bf16[48,768]{1,0:T(8,128)(2,1)S(1)}, bf16[48,768]{1,0:T(8,128)(2,1)S(1)}, u32[]{:S(2)}, u32[]{:S(2)}) collective-permute-start(bf16[48,768]{1,0:T(8,128)(2,1)S(1)} %collective-permute-done.3.refs_3_), channel_id=1, source_target_pairs={{0,8},{8,0},{16,24},{24,16},{32,40},{40,32},{48,56},{56,48},{64,72... | collective-permute-start | bytes 221192 | tf_op jit(solution)/shard_map/ppermute | solution.py:72
  42.1 1.0 %copy-start = (bf16[768,768]{1,0:T(8,128)(2,1)}, bf16[768,768]{1,0:T(8,128)(2,1)S(1)}, u32[]{:S(2)}) copy-start(bf16[768,768]{1,0:T(8,128)(2,1)S(1)} %assemble.1.virt_ref) | copy-start | bytes 3538948
  57.6 1.0 %copy-start.3 = (bf16[32,24,768]{2,1,0:T(8,128)(2,1)}, bf16[32,24,768]{2,1,0:T(8,128)(2,1)S(1)}, u32[]{:S(2)}) copy-start(bf16[32,24,768]{2,1,0:T(8,128)(2,1)S(1)} %all-to-all-done.1.returned_ref) | copy-start | bytes 3538948

commit v3 on v2

--- a/solution.py
+++ b/solution.py
@@ -11,11 +11,12 @@
 LANES = 128
 SCREEN_FLOPS = 1000
 ALL_VMEM = 60 * 1024 * 1024
-MOST_VMEM = 57 * 1024 * 1024
+MOST_VMEM = 48 * 1024 * 1024
 WIDE_VMEM = 10 * 1024 * 1024
 PART = 64
 SMALL_VMEM = 4 * 1024 * 1024
 VMEM = pl.BlockSpec(memory_space=pltpu.VMEM)
+ANY = pl.BlockSpec(memory_space=pl.ANY)
 
 
 def expand(occupancy, rows, cols):
@@ -27,25 +28,56 @@
     return jnp.concatenate([jnp.broadcast_to(wide[i : i + 1], (BLK, cols)) for i in range(rows // BLK)], axis=0)
 
 
-def screen_kernel(coulomb_ref, occupancy_ref, out_ref):
-    rows, cols = coulomb_ref.shape[1:]
-    mask = expand(occupancy_ref[...], rows, cols).astype(coulomb_ref.dtype)
-    out_ref[...] = coulomb_ref[...] * mask[None]
-
-
-def screen(coulomb_blocks, occupancy, share):
-    rows, cols = coulomb_blocks.shape[1:]
+def screen_kernel(coulomb_ref, occupancy_ref, out_ref, part, occupancy, in_sem, out_sem, occupancy_sem):
+    share, rows, cols = part.shape
+    chunks = in_sem.shape[0]
+    block = share // chunks
+    first = lax.axis_index("aux") * share
+
+    def fetch(i):
+        return pltpu.make_async_copy(
+            coulomb_ref.at[pl.ds(first + i * block, block)], part.at[pl.ds(i * block, block)], in_sem.at[i]
+        )
+
+    def put(i):
+        here = pl.ds(i * block, block)
+        return pltpu.make_async_copy(part.at[here], out_ref.at[here], out_sem.at[i])
+
+    copy = pltpu.make_async_copy(occupancy_ref, occupancy, occupancy_sem)
+    copy.start()
+    for i in range(chunks):
+        fetch(i).start()
+    copy.wait()
+    mask = expand(occupancy[...], rows, cols).astype(part.dtype)
+
+    @pl.loop(0, chunks)
+    def _(i):
+        fetch(i).wait()
+        here = pl.ds(i * block, block)
+        part[here] = part[here] * mask[None]
+        put(i).start()
+
+    @pl.loop(0, chunks)
+    def _(i):
+        put(i).wait()
+
+
+def screen(coulomb_blocks, occupancy, share, chunks=4):
+    part = (share, *coulomb_blocks.shape[1:])
+    dtype = coulomb_blocks.dtype
     return pl.pallas_call(
         screen_kernel,
-        grid=(1,),
-        in_specs=[
-            pl.BlockSpec((share, rows, cols), lambda i: (lax.axis_index("aux"), 0, 0)),
-            pl.BlockSpec(occupancy.shape, lambda i: (0, 0)),
+        in_specs=[ANY, ANY],
+        out_specs=ANY,
+        out_shape=jax.ShapeDtypeStruct(part, dtype),
+        scratch_shapes=[
+            pltpu.VMEM(part, dtype),
+            pltpu.VMEM(occupancy.shape, occupancy.dtype),
+            pltpu.SemaphoreType.DMA((chunks,)),
+            pltpu.SemaphoreType.DMA((chunks,)),
+            pltpu.SemaphoreType.DMA,
         ],
-        out_specs=pl.BlockSpec((share, rows, cols), lambda i: (0, 0, 0)),
-        out_shape=jax.ShapeDtypeStruct((share, rows, cols), coulomb_blocks.dtype),
         compiler_params=pltpu.CompilerParams(vmem_limit_bytes=ALL_VMEM),
-        cost_estimate=pl.CostEstimate(flops=SCREEN_FLOPS, bytes_accessed=0, transcendentals=0),
         name="screen",
     )(coulomb_blocks, occupancy)
 
@@ -129,23 +161,35 @@
             pl.BlockSpec(occupancy.shape, lambda i: (0, 0)),
         ],
         out_specs=pl.BlockSpec((rows, count, cols), lambda i: (0, i, 0)),
-        out_shape=jax.ShapeDtypeStruct((rows, naux, cols), dtype),
+        out_shape=jax.ShapeDtypeStruct((2 * rows, naux, cols), dtype),
         scratch_shapes=[pltpu.VMEM((2 * rows, cols), dtype)],
         compiler_params=pltpu.CompilerParams(vmem_limit_bytes=ALL_VMEM),
         name="apply_virt",
     )(coulomb_blocks.reshape(naux * rows, cols), virt_t, occupancy)
 
 
-def apply_occ_kernel(occ_ref, screened_ref, out_ref):
-    out_ref[...] = jnp.dot(occ_ref[...], screened_ref[...], preferred_element_type=jnp.float32).astype(out_ref.dtype)
-
-
-def apply_occ(green_occ, screened):
+def apply_occ_kernel(occ_ref, screened_ref, out_ref, half, sem):
+    chunks = sem.shape[0]
+    block = half.shape[0] // chunks
+    copies = []
+    for i in range(chunks):
+        here = pl.ds(i * block, block)
+        half[here, :] = jnp.dot(
+            occ_ref[here, :], screened_ref[...], preferred_element_type=jnp.float32
+        ).astype(half.dtype)
+        copies.append(pltpu.make_async_copy(half.at[here], out_ref.at[here], sem.at[i]))
+        copies[-1].start()
+    for copy in copies:
+        copy.wait()
+
+
+def apply_occ(green_occ, screened, chunks=3):
     return pl.pallas_call(
         apply_occ_kernel,
         in_specs=[VMEM] * 2,
-        out_specs=VMEM,
+        out_specs=ANY,
         out_shape=jax.ShapeDtypeStruct(screened.shape, screened.dtype),
+        scratch_shapes=[pltpu.VMEM(screened.shape, screened.dtype), pltpu.SemaphoreType.DMA((chunks,))],
         compiler_params=pltpu.CompilerParams(vmem_limit_bytes=WIDE_VMEM),
         name="apply_occ",
     )(green_occ, screened)
@@ -183,12 +227,12 @@
 
 
 def contract(half_rows, returned, chunks=4):
-    rows, naux, cols = half_rows.shape
-    share = returned.shape[0]
+    _, naux, cols = half_rows.shape
+    share, rows, _ = returned.shape
     dtype = half_rows.dtype
     return pl.pallas_call(
         contract_kernel,
-        in_specs=[VMEM, pl.BlockSpec(memory_space=pl.ANY)],
+        in_specs=[VMEM, ANY],
         out_specs=VMEM,
         out_shape=jax.ShapeDtypeStruct((naux, LANES), jnp.float32),
         scratch_shapes=[
@@ -201,18 +245,8 @@
     )(returned, half_rows)
 
 
-def finish_kernel(parts_ref, out_ref):
-    out_ref[...] = jnp.sum(parts_ref[...], axis=0)[:, : out_ref.shape[1]]
-
-
 def finish(parts, share):
-    return pl.pallas_call(
-        finish_kernel,
-        in_specs=[VMEM],
-        out_specs=pl.BlockSpec((parts.shape[1], share), lambda: (0, 0)),
-        out_shape=jax.ShapeDtypeStruct((parts.shape[1], share), parts.dtype),
-        name="finish",
-    )(parts)
+    return jnp.sum(parts[:, :, :share], axis=0)
 
 
 def shards(coulomb_blocks, occupancy, green_occ, green_virt):

time: 80.9 us -> 76.2 us (0.942)
  Pallas kernels: 25.8 us -> 21.6 us
  local copies, waits for them, and re-layouts: 2.06 us -> 1.04 us
    pallas_call x4 -> x3, Pallas kernels: 12.8 us -> 8.67 us  [the longest x1 4.7 us: contract(): pl.pallas_call(contract_kernel, in_specs=[VMEM, ANY], out_specs=VMEM, out...]
    unnamed x8 -> x6, local copies, waits for them, and re-layouts: 2.05 us -> 1.04 us
  transfers between devices with their start and end apart: 10 -> 10, of which waited for: 4 -> 4; matrix products, arithmetic and copies ran while one was open for 0% -> 0% of each run, Pallas kernels for 19% -> 20%
where the time goes in v3:
time: 76.2 us; the launch traced here: 75.8 us
  starting transfers between devices  26 us (34%)
  Pallas kernels  21.6 us (28%)
  waiting for transfers between devices  13.2 us (17%)
  blocking collectives  13.2 us (17%)
  local copies, waits for them, and re-layouts  1.04 us (1%)
    all_to_all x1, blocking collectives, shards(): lax.all_to_all(parts, 'orb', split_axis=0, concat_axis=0, tiled=True)  13.2 us
    pallas_call x1, Pallas kernels, apply_virt(): pl.pallas_call(apply_virt_kernel, grid=(naux // count,), in_specs=[pl.Blo...  12.9 us
    ppermute x4, starting transfers between devices, fetch_virt(): lax.ppermute(own if 2 * dist < ranks else own_half, ('orb', 'aux'), pairs)  9.01 us
    all_to_all x1, waiting for transfers between devices, shards(): lax.all_to_all(own, 'orb', split_axis=0, concat_axis=0, tiled=True)  8.96 us
    all_to_all x1, starting transfers between devices, shards(): lax.all_to_all(own, 'orb', split_axis=0, concat_axis=0, tiled=True)  8.73 us
    all_to_all x1, starting transfers between devices, shards(): lax.all_to_all(half_occ.reshape(ranks, mu_rows, nao), 'orb', split_axis=0...  7.14 us
    pallas_call x1, Pallas kernels, contract(): pl.pallas_call(contract_kernel, in_specs=[VMEM, ANY], out_specs=VMEM, out...  4.7 us
    pallas_call x1, Pallas kernels, screen(): pl.pallas_call(screen_kernel, in_specs=[ANY, ANY], out_specs=ANY, out_sha...  2.11 us
  transfers between devices with their start and end apart: 10, of which 4 were waited for; matrix products, arithmetic and copies ran while one was open for 0% of the time, Pallas kernels for 20%

profile of v3, /device:TPU:1, one launch (start us, length us, event | category | flops | bytes accessed | tf_op | source)
XLA Modules:
  0.0 75.8 jit_solution(17780706541370847973)
XLA Ops:
  0.0 2.1 %screen.1 = bf16[32,24,768]{2,1,0:T(8,128)(2,1)} custom-call(bf16[256,24,768]{2,1,0:T(8,128)(2,1)} %coulomb_ref.1, s32[3,96]{1,0:T(4,128)} %occupancy_ref.3), custom_call_target="tpu_custom_call" | custom-call | tf_op jit(solution)/shard_map/screen/pallas_call | solution.py:68
  2.1 0.0 copy-start.2
  2.1 0.0 copy-start.1
  2.1 8.7 %all-to-all-start = ((bf16[32,24,768]{2,1,0:T(8,128)(2,1)}), bf16[32,24,768]{2,1,0:T(8,128)(2,1)S(1)}, u32[]{:S(2)}, u32[]{:S(2)}) async-start(bf16[32,24,768]{2,1,0:T(8,128)(2,1)} %screen.1), calls=%async_computation | async-start | bytes 2359296 | tf_op jit(solution)/shard_map/all_to_all | solution.py:259
  10.9 0.0 copy-done.2
  10.9 4.4 %collective-permute-start.2 = (bf16[96,768]{1,0:T(8,128)(2,1)S(1)}, bf16[96,768]{1,0:T(8,128)(2,1)S(1)}, u32[]{:S(2)}, u32[]{:S(2)}) collective-permute-start(bf16[96,768]{1,0:T(8,128)(2,1)S(1)} %bitcast.10), channel_id=1, source_target_pairs={{0,5},{1,6},{2,7},{3,0},{4,1},{5,2},{6,3},{7,4},{8,11},{9,12},{10,... | collective-permute-start | bytes 442376 | tf_op jit(solution)/shard_map/ppermute | solution.py:98
  15.3 3.3 %collective-permute-start.1 = (bf16[96,768]{1,0:T(8,128)(2,1)S(1)}, bf16[96,768]{1,0:T(8,128)(2,1)S(1)}, u32[]{:S(2)}, u32[]{:S(2)}) collective-permute-start(bf16[96,768]{1,0:T(8,128)(2,1)S(1)} %bitcast.11), channel_id=1, source_target_pairs={{0,6},{1,7},{2,0},{3,1},{4,2},{5,3},{6,4},{7,5},{8,10},{9,11},{10,... | collective-permute-start | bytes 442376 | tf_op jit(solution)/shard_map/ppermute | solution.py:98
  18.6 0.7 collective-permute-start
  19.4 0.5 collective-permute-start.3
  19.9 9.0 %all-to-all-done = bf16[32,24,768]{2,1,0:T(8,128)(2,1)S(1)} async-done(((bf16[32,24,768]{2,1,0:T(8,128)(2,1)}), bf16[32,24,768]{2,1,0:T(8,128)(2,1)S(1)}, u32[]{:S(2)}, u32[]{:S(2)}) %all-to-all-start) | async-done | bytes 1179680 | tf_op jit(solution)/shard_map/all_to_all | solution.py:259
  28.9 0.0 copy-done.1
  28.9 1.9 %apply_occ.1 = bf16[768,768]{1,0:T(8,128)(2,1)} custom-call(bf16[768,768]{1,0:T(8,128)(2,1)S(1)} %copy-done.1, bf16[768,768]{1,0:T(8,128)(2,1)S(1)} %bitcast.8), custom_call_target="tpu_custom_call" | custom-call | tf_op jit(solution)/shard_map/apply_occ/pallas_call | solution.py:187
  30.7 1.6 %collective-permute-done.3.refs_3_ = bf16[48,768]{1,0:T(8,128)(2,1)S(1)} collective-permute-done((bf16[48,768]{1,0:T(8,128)(2,1)S(1)}, bf16[48,768]{1,0:T(8,128)(2,1)S(1)}, u32[]{:S(2)}, u32[]{:S(2)}) %collective-permute-start.3) | collective-permute-done | bytes 73760 | tf_op jit(solution)/shard_map/ppermute | solution.py:98
  32.4 0.0 collective-permute-done.2.refs_2_
  32.4 0.0 collective-permute-done.1.refs_1_
  32.4 0.0 collective-permute-done.refs_0_
  32.4 7.1 %all-to-all-start.1 = ((bf16[32,24,768]{2,1,0:T(8,128)(2,1)}), bf16[32,24,768]{2,1,0:T(8,128)(2,1)S(1)}, u32[]{:S(2)}, u32[]{:S(2)}) async-start(bf16[32,24,768]{2,1,0:T(8,128)(2,1)} %bitcast.3), calls=%async_computation.1 | async-start | bytes 2359296 | tf_op jit(solution)/shard_map/all_to_all | solution.py:264
  39.5 0.3 collective-permute-start.4
  39.9 0.3 collective-permute-start.5
  40.1 0.2 collective-permute-start.6
  40.4 0.3 collective-permute-start.7
  40.6 1.0 %collective-permute-done.7.refs_7_ = bf16[48,768]{1,0:T(8,128)(2,1)S(1)} collective-permute-done((bf16[48,768]{1,0:T(8,128)(2,1)S(1)}, bf16[48,768]{1,0:T(8,128)(2,1)S(1)}, u32[]{:S(2)}, u32[]{:S(2)}) %collective-permute-start.7) | collective-permute-done | bytes 73760 | tf_op jit(solution)/shard_map/ppermute | solution.py:104
  41.6 0.0 collective-permute-done.4.refs_4_
  41.6 0.0 collective-permute-done.5.refs_5_
  41.6 0.0 collective-permute-done.6.refs_6_
  41.6 0.1 assemble.1.virt_ref
  41.7 0.0 copy-start
  41.8 1.0 %copy-done = bf16[768,768]{1,0:T(8,128)(2,1)} copy-done((bf16[768,768]{1,0:T(8,128)(2,1)}, bf16[768,768]{1,0:T(8,128)(2,1)S(1)}, u32[]{:S(2)}) %copy-start) | copy-done | bytes 1179672
  42.8 12.9 %apply_virt.1.half_ref = bf16[48,256,768]{2,1,0:T(8,128)(2,1)} custom-call(bf16[6144,768]{1,0:T(8,128)(2,1)} %bitcast.14, bf16[768,768]{1,0:T(8,128)(2,1)} %copy-done, s32[3,96]{1,0:T(4,128)} %occupancy_ref.3), custom_call_target="tpu_custom_call" | custom-call | tf_op jit(solution)/shard_map/apply_virt/pallas_call | solution.py:155
  55.7 1.6 %all-to-all-done.1.returned_ref = bf16[32,24,768]{2,1,0:T(8,128)(2,1)S(1)} async-done(((bf16[32,24,768]{2,1,0:T(8,128)(2,1)}), bf16[32,24,768]{2,1,0:T(8,128)(2,1)S(1)}, u32[]{:S(2)}, u32[]{:S(2)}) %all-to-all-start.1) | async-done | bytes 1179680 | tf_op jit(solution)/shard_map/all_to_all | solution.py:264
  57.2 4.7 %contract.1 = f32[256,128]{1,0:T(8,128)S(1)} custom-call(bf16[32,24,768]{2,1,0:T(8,128)(2,1)S(1)} %all-to-all-done.1.returned_ref, bf16[48,256,768]{2,1,0:T(8,128)(2,1)} %apply_virt.1.half_ref), custom_call_target="tpu_custom_call" | custom-call | tf_op jit(solution)/shard_map/contract/pallas_call | solution.py:233
  61.9 13.2 %all_to_all.15 = f32[32,8,128]{2,1,0:T(8,128)S(1)} all-to-all(f32[32,8,128]{2,1,0:T(8,128)S(1)} %bitcast.9), channel_id=1, replica_groups=mesh['orb'=32,'aux'=8] {'orb'}, dimensions={0} | all-to-all | bytes 262144 | tf_op jit(solution)/shard_map/all_to_all | solution.py:267
  75.2 0.6 slice_reduce_fusion
  (1 shorter events, 0.0 us)
Async XLA Ops:
  2.1 8.8 %copy-start.2 = (bf16[768,96]{0,1:T(8,128)(2,1)S(1)}, bf16[768,96]{0,1:T(8,128)(2,1)}, u32[]{:S(2)}) copy-start(bf16[768,96]{0,1:T(8,128)(2,1)} %param.7) | copy-start | bytes 442372
  2.1 26.7 %copy-start.1 = (bf16[768,768]{1,0:T(8,128)(2,1)S(1)}, bf16[768,768]{1,0:T(8,128)(2,1)}, u32[]{:S(2)}) copy-start(bf16[768,768]{1,0:T(8,128)(2,1)} %occ_ref.1) | copy-start | bytes 3538948
  2.1 26.7 %all-to-all-start = ((bf16[32,24,768]{2,1,0:T(8,128)(2,1)}), bf16[32,24,768]{2,1,0:T(8,128)(2,1)S(1)}, u32[]{:S(2)}, u32[]{:S(2)}) async-start(bf16[32,24,768]{2,1,0:T(8,128)(2,1)} %screen.1), calls=%async_computation | async-start | bytes 2359296 | tf_op jit(solution)/shard_map/all_to_all | solution.py:259
  10.9 21.5 %collective-permute-start.2 = (bf16[96,768]{1,0:T(8,128)(2,1)S(1)}, bf16[96,768]{1,0:T(8,128)(2,1)S(1)}, u32[]{:S(2)}, u32[]{:S(2)}) collective-permute-start(bf16[96,768]{1,0:T(8,128)(2,1)S(1)} %bitcast.10), channel_id=1, source_target_pairs={{0,5},{1,6},{2,7},{3,0},{4,1},{5,2},{6,3},{7,4},{8,11},{9,12},{10,... | collective-permute-start | bytes 442376 | tf_op jit(solution)/shard_map/ppermute | solution.py:98
  15.3 17.1 %collective-permute-start.1 = (bf16[96,768]{1,0:T(8,128)(2,1)S(1)}, bf16[96,768]{1,0:T(8,128)(2,1)S(1)}, u32[]{:S(2)}, u32[]{:S(2)}) collective-permute-start(bf16[96,768]{1,0:T(8,128)(2,1)S(1)} %bitcast.11), channel_id=1, source_target_pairs={{0,6},{1,7},{2,0},{3,1},{4,2},{5,3},{6,4},{7,5},{8,10},{9,11},{10,... | collective-permute-start | bytes 442376 | tf_op jit(solution)/shard_map/ppermute | solution.py:98
  18.6 13.8 %collective-permute-start = (bf16[96,768]{1,0:T(8,128)(2,1)S(1)}, bf16[96,768]{1,0:T(8,128)(2,1)S(1)}, u32[]{:S(2)}, u32[]{:S(2)}) collective-permute-start(bf16[96,768]{1,0:T(8,128)(2,1)S(1)} %bitcast.12), channel_id=1, source_target_pairs={{0,7},{1,0},{2,1},{3,2},{4,3},{5,4},{6,5},{7,6},{8,9},{9,10},{10,1... | collective-permute-start | bytes 442376 | tf_op jit(solution)/shard_map/ppermute | solution.py:98
  19.4 13.0 %collective-permute-start.3 = (bf16[48,768]{1,0:T(8,128)(2,1)S(1)}, bf16[48,768]{1,0:T(8,128)(2,1)S(1)}, u32[]{:S(2)}, u32[]{:S(2)}) collective-permute-start(bf16[48,768]{1,0:T(8,128)(2,1)S(1)} %dynamic-slice_bitcast_fusion), channel_id=1, source_target_pairs={{0,4},{1,5},{2,6},{3,7},{4,0},{5,1},{6,2},{7,3},{8,12},{9,13},{10,... | collective-permute-start | bytes 221192 | tf_op jit(solution)/shard_map/ppermute | solution.py:98
  32.4 24.8 %all-to-all-start.1 = ((bf16[32,24,768]{2,1,0:T(8,128)(2,1)}), bf16[32,24,768]{2,1,0:T(8,128)(2,1)S(1)}, u32[]{:S(2)}, u32[]{:S(2)}) async-start(bf16[32,24,768]{2,1,0:T(8,128)(2,1)} %bitcast.3), calls=%async_computation.1 | async-start | bytes 2359296 | tf_op jit(solution)/shard_map/all_to_all | solution.py:264
  39.5 2.1 %collective-permute-start.4 = (bf16[96,768]{1,0:T(8,128)(2,1)S(1)}, bf16[96,768]{1,0:T(8,128)(2,1)S(1)}, u32[]{:S(2)}, u32[]{:S(2)}) collective-permute-start(bf16[96,768]{1,0:T(8,128)(2,1)S(1)} %collective-permute-done.refs_0_), channel_id=1, source_target_pairs={{0,8},{8,0},{16,24},{24,16},{32,40},{40,32},{48,56},{56,48},{64,72... | collective-permute-start | bytes 442376 | tf_op jit(solution)/shard_map/ppermute | solution.py:104
  39.9 1.8 %collective-permute-start.5 = (bf16[96,768]{1,0:T(8,128)(2,1)S(1)}, bf16[96,768]{1,0:T(8,128)(2,1)S(1)}, u32[]{:S(2)}, u32[]{:S(2)}) collective-permute-start(bf16[96,768]{1,0:T(8,128)(2,1)S(1)} %collective-permute-done.1.refs_1_), channel_id=1, source_target_pairs={{0,8},{8,0},{16,24},{24,16},{32,40},{40,32},{48,56},{56,48},{64,72... | collective-permute-start | bytes 442376 | tf_op jit(solution)/shard_map/ppermute | solution.py:104
  40.1 1.5 %collective-permute-start.6 = (bf16[96,768]{1,0:T(8,128)(2,1)S(1)}, bf16[96,768]{1,0:T(8,128)(2,1)S(1)}, u32[]{:S(2)}, u32[]{:S(2)}) collective-permute-start(bf16[96,768]{1,0:T(8,128)(2,1)S(1)} %collective-permute-done.2.refs_2_), channel_id=1, source_target_pairs={{0,8},{8,0},{16,24},{24,16},{32,40},{40,32},{48,56},{56,48},{64,72... | collective-permute-start | bytes 442376 | tf_op jit(solution)/shard_map/ppermute | solution.py:104
  40.4 1.3 %collective-permute-start.7 = (bf16[48,768]{1,0:T(8,128)(2,1)S(1)}, bf16[48,768]{1,0:T(8,128)(2,1)S(1)}, u32[]{:S(2)}, u32[]{:S(2)}) collective-permute-start(bf16[48,768]{1,0:T(8,128)(2,1)S(1)} %collective-permute-done.3.refs_3_), channel_id=1, source_target_pairs={{0,8},{8,0},{16,24},{24,16},{32,40},{40,32},{48,56},{56,48},{64,72... | collective-permute-start | bytes 221192 | tf_op jit(solution)/shard_map/ppermute | solution.py:104
  41.7 1.0 %copy-start = (bf16[768,768]{1,0:T(8,128)(2,1)}, bf16[768,768]{1,0:T(8,128)(2,1)S(1)}, u32[]{:S(2)}) copy-start(bf16[768,768]{1,0:T(8,128)(2,1)S(1)} %assemble.1.virt_ref) | copy-start | bytes 3538948

commit v4 on v3

--- a/solution.py
+++ b/solution.py
@@ -14,7 +14,7 @@
 MOST_VMEM = 48 * 1024 * 1024
 WIDE_VMEM = 10 * 1024 * 1024
 PART = 64
-SMALL_VMEM = 4 * 1024 * 1024
+PRODUCT_VMEM = 56 * 1024 * 1024
 VMEM = pl.BlockSpec(memory_space=pltpu.VMEM)
 ANY = pl.BlockSpec(memory_space=pl.ANY)
 
@@ -88,15 +88,15 @@
     own = green_virt.T
     half = own.shape[0] // 2
     own_half = lax.dynamic_slice_in_dim(own, lax.rem(lax.axis_index("orb"), 2) * half, half, 0)
-    got = []
-    for dist in range(1, ranks // 2 + 1):
+    got = {}
+    for dist in range(ranks // 2, 0, -1):
         pairs = []
         for orb in range(orbs):
             for aux in range(ranks):
                 target = (aux - dist if orb % 2 == 0 else aux + dist) % ranks
                 pairs.append((orb * ranks + aux, orb * ranks + target))
-        got.append(lax.ppermute(own if 2 * dist < ranks else own_half, ("orb", "aux"), pairs))
-    return own, got
+        got[dist] = lax.ppermute(own if 2 * dist < ranks else own_half, ("orb", "aux"), pairs)
+    return own, [got[dist] for dist in sorted(got)]
 
 
 def swap_cores(blocks):
@@ -104,68 +104,57 @@
     return [lax.ppermute(block, "orb", pairs) for block in blocks]
 
 
-def assemble_kernel(ranks, own_ref, *refs):
-    (*block_refs, out_ref) = refs
+def assemble(ranks, own_ref, block_refs, virt):
     me, side = lax.axis_index("aux"), lax.rem(lax.axis_index("orb"), 2)
     cols = own_ref.shape[0]
     far = ranks // 2
-    out_ref[pl.ds(pl.multiple_of(me * cols, cols), cols), :] = own_ref[...]
+    virt[pl.ds(pl.multiple_of(me * cols, cols), cols), :] = own_ref[...]
     for which in range(2):
         core = side if which == 0 else 1 - side
         for dist in range(1, far + 1):
             ref = block_refs[which * far + dist - 1]
             source = lax.rem(me + ranks + jnp.where(core == 0, dist, -dist), ranks)
             first = source * cols + (core * (cols // 2) if 2 * dist == ranks else 0)
-            out_ref[pl.ds(pl.multiple_of(first, cols // 2), ref.shape[0]), :] = ref[...]
-
-
-def assemble(own, got, other):
-    ranks = lax.axis_size("aux")
-    blocks = [*got, *other]
-    return pl.pallas_call(
-        functools.partial(assemble_kernel, ranks),
-        in_specs=[VMEM] * (1 + len(blocks)),
-        out_specs=VMEM,
-        out_shape=jax.ShapeDtypeStruct((ranks * own.shape[0], own.shape[1]), own.dtype),
-        compiler_params=pltpu.CompilerParams(vmem_limit_bytes=SMALL_VMEM),
-        name="assemble",
-    )(own, *blocks)
-
-
-def apply_virt_kernel(coulomb_ref, virt_ref, occupancy_ref, out_ref, mask):
+            virt[pl.ds(pl.multiple_of(first, cols // 2), ref.shape[0]), :] = ref[...]
+
+
+def apply_virt_kernel(ranks, coulomb_ref, occupancy_ref, own_ref, *refs):
+    (*block_refs, out_ref, virt, mask) = refs
     rows, count, cols = out_ref.shape
 
     @pl.when(pl.program_id(0) == 0)
     def _():
         once = expand(occupancy_ref[...], rows, cols)
         mask[...] = jnp.concatenate([once, once], axis=0).astype(mask.dtype)
+        assemble(ranks, own_ref, block_refs, virt)
 
     @pl.loop(0, count // PART)
     def _(i):
         here = pl.ds(pl.multiple_of(i * PART * rows, PART * rows), PART * rows)
         screened = coulomb_ref[here, :].reshape(PART // 2, 2 * rows, cols) * mask[...][None]
-        half = jnp.dot(screened.reshape(PART * rows, cols), virt_ref[...], preferred_element_type=jnp.float32)
+        half = jnp.dot(screened.reshape(PART * rows, cols), virt[...], preferred_element_type=jnp.float32)
         half = half.reshape(PART, rows, cols).astype(out_ref.dtype)
         out_ref[:, pl.ds(pl.multiple_of(i * PART, PART), PART), :] = jnp.swapaxes(half, 0, 1)
 
 
-def apply_virt(coulomb_blocks, virt_t, occupancy, count=64):
+def apply_virt(coulomb_blocks, occupancy, own, blocks, count=64):
     naux, rows, cols = coulomb_blocks.shape
     dtype = coulomb_blocks.dtype
-    return pl.pallas_call(
-        apply_virt_kernel,
+    ranks = lax.axis_size("aux")
+    return pl.pallas_call(
+        functools.partial(apply_virt_kernel, ranks),
         grid=(naux // count,),
         in_specs=[
             pl.BlockSpec((count * rows, cols), lambda i: (i, 0)),
-            pl.BlockSpec(virt_t.shape, lambda i: (0, 0)),
             pl.BlockSpec(occupancy.shape, lambda i: (0, 0)),
+            *[VMEM] * (1 + len(blocks)),
         ],
         out_specs=pl.BlockSpec((rows, count, cols), lambda i: (0, i, 0)),
         out_shape=jax.ShapeDtypeStruct((2 * rows, naux, cols), dtype),
-        scratch_shapes=[pltpu.VMEM((2 * rows, cols), dtype)],
-        compiler_params=pltpu.CompilerParams(vmem_limit_bytes=ALL_VMEM),
+        scratch_shapes=[pltpu.VMEM((ranks * own.shape[0], cols), dtype), pltpu.VMEM((2 * rows, cols), dtype)],
+        compiler_params=pltpu.CompilerParams(vmem_limit_bytes=PRODUCT_VMEM),
         name="apply_virt",
-    )(coulomb_blocks.reshape(naux * rows, cols), virt_t, occupancy)
+    )(coulomb_blocks.reshape(naux * rows, cols), occupancy, own, *blocks)
 
 
 def apply_occ_kernel(occ_ref, screened_ref, out_ref, half, sem):
@@ -258,9 +247,8 @@
     own_virt, got = fetch_virt(green_virt)
     screened = lax.all_to_all(own, "orb", split_axis=0, concat_axis=0, tiled=True).reshape(nao, nao)
     half_occ = apply_occ(green_occ, screened)
-    half_occ, *got = lax.optimization_barrier((half_occ, *got))
-    virt_t = assemble(own_virt, got, swap_cores(got))
-    half_rows = apply_virt(coulomb_blocks, virt_t, occupancy)
+    half_occ, *late = lax.optimization_barrier((half_occ, *got))
+    half_rows = apply_virt(coulomb_blocks, occupancy, own_virt, [*late, *swap_cores(late)])
     returned = lax.all_to_all(half_occ.reshape(ranks, mu_rows, nao), "orb", split_axis=0, concat_axis=0, tiled=True)
     partial_pol = contract(half_rows, returned)
     parts = partial_pol.reshape(ranks, naux // ranks, LANES)

time: 76.2 us -> 76 us (level)
    pallas_call x2 -> x1, Pallas kernels: 13 us -> 12.9 us  [apply_virt(): pl.pallas_call(functools.partial(apply_virt_kernel, ranks), grid=(naux //...]
where the time goes in v4:
time: 76 us; the launch traced here: 75.6 us
  starting transfers between devices  26 us (34%)
  Pallas kernels  21.7 us (29%)
  waiting for transfers between devices  13.4 us (18%)
  blocking collectives  13 us (17%)
  local copies, waits for them, and re-layouts  0.78 us (1%)
    all_to_all x1, blocking collectives, shards(): lax.all_to_all(parts, 'orb', split_axis=0, concat_axis=0, tiled=True)  13 us
    pallas_call x1, Pallas kernels, apply_virt(): pl.pallas_call(functools.partial(apply_virt_kernel, ranks), grid=(naux //...  12.9 us
    ppermute x4, starting transfers between devices, fetch_virt(): lax.ppermute(own if 2 * dist < ranks else own_half, ('orb', 'aux'), pairs)  9.01 us
    all_to_all x1, waiting for transfers between devices, shards(): lax.all_to_all(own, 'orb', split_axis=0, concat_axis=0, tiled=True)  8.96 us
    all_to_all x1, starting transfers between devices, shards(): lax.all_to_all(own, 'orb', split_axis=0, concat_axis=0, tiled=True)  8.73 us
    all_to_all x1, starting transfers between devices, shards(): lax.all_to_all(half_occ.reshape(ranks, mu_rows, nao), 'orb', split_axis=0...  7.15 us
    pallas_call x1, Pallas kernels, contract(): pl.pallas_call(contract_kernel, in_specs=[VMEM, ANY], out_specs=VMEM, out...  4.72 us
    pallas_call x1, Pallas kernels, screen(): pl.pallas_call(screen_kernel, in_specs=[ANY, ANY], out_specs=ANY, out_sha...  2.13 us
  transfers between devices with their start and end apart: 10, of which 4 were waited for; matrix products, arithmetic and copies ran while one was open for 0% of the time, Pallas kernels for 20%

profile of v4, /device:TPU:1, one launch (start us, length us, event | category | flops | bytes accessed | tf_op | source)
XLA Modules:
  0.0 75.6 jit_solution(15947260729611121414)
XLA Ops:
  0.0 2.1 %screen.1 = bf16[32,24,768]{2,1,0:T(8,128)(2,1)} custom-call(bf16[256,24,768]{2,1,0:T(8,128)(2,1)} %coulomb_ref.1, s32[3,96]{1,0:T(4,128)} %occupancy_ref.3), custom_call_target="tpu_custom_call" | custom-call | tf_op jit(solution)/shard_map/screen/pallas_call | solution.py:68
  2.1 0.0 copy-start.1
  2.1 0.0 copy-start
  2.2 8.7 %all-to-all-start = ((bf16[32,24,768]{2,1,0:T(8,128)(2,1)}), bf16[32,24,768]{2,1,0:T(8,128)(2,1)S(1)}, u32[]{:S(2)}, u32[]{:S(2)}) async-start(bf16[32,24,768]{2,1,0:T(8,128)(2,1)} %screen.1), calls=%async_computation | async-start | bytes 2359296 | tf_op jit(solution)/shard_map/all_to_all | solution.py:248
  10.9 0.0 copy-done.1
  10.9 4.4 %collective-permute-start.2 = (bf16[96,768]{1,0:T(8,128)(2,1)S(1)}, bf16[96,768]{1,0:T(8,128)(2,1)S(1)}, u32[]{:S(2)}, u32[]{:S(2)}) collective-permute-start(bf16[96,768]{1,0:T(8,128)(2,1)S(1)} %bitcast.12), channel_id=1, source_target_pairs={{0,5},{1,6},{2,7},{3,0},{4,1},{5,2},{6,3},{7,4},{8,11},{9,12},{10,... | collective-permute-start | bytes 442376 | tf_op jit(solution)/shard_map/ppermute | solution.py:98
  15.3 3.3 %collective-permute-start.1 = (bf16[96,768]{1,0:T(8,128)(2,1)S(1)}, bf16[96,768]{1,0:T(8,128)(2,1)S(1)}, u32[]{:S(2)}, u32[]{:S(2)}) collective-permute-start(bf16[96,768]{1,0:T(8,128)(2,1)S(1)} %bitcast.13), channel_id=1, source_target_pairs={{0,6},{1,7},{2,0},{3,1},{4,2},{5,3},{6,4},{7,5},{8,10},{9,11},{10,... | collective-permute-start | bytes 442376 | tf_op jit(solution)/shard_map/ppermute | solution.py:98
  18.6 0.7 collective-permute-start
  19.4 0.5 collective-permute-start.3
  19.9 9.0 %all-to-all-done = bf16[32,24,768]{2,1,0:T(8,128)(2,1)S(1)} async-done(((bf16[32,24,768]{2,1,0:T(8,128)(2,1)}), bf16[32,24,768]{2,1,0:T(8,128)(2,1)S(1)}, u32[]{:S(2)}, u32[]{:S(2)}) %all-to-all-start) | async-done | bytes 1179680 | tf_op jit(solution)/shard_map/all_to_all | solution.py:248
  28.9 0.0 copy-done
  28.9 1.9 %apply_occ.1 = bf16[768,768]{1,0:T(8,128)(2,1)} custom-call(bf16[768,768]{1,0:T(8,128)(2,1)S(1)} %copy-done, bf16[768,768]{1,0:T(8,128)(2,1)S(1)} %bitcast.8), custom_call_target="tpu_custom_call" | custom-call | tf_op jit(solution)/shard_map/apply_occ/pallas_call | solution.py:176
  30.8 1.6 %collective-permute-done.3.refs_3_ = bf16[48,768]{1,0:T(8,128)(2,1)S(1)} collective-permute-done((bf16[48,768]{1,0:T(8,128)(2,1)S(1)}, bf16[48,768]{1,0:T(8,128)(2,1)S(1)}, u32[]{:S(2)}, u32[]{:S(2)}) %collective-permute-start.3) | collective-permute-done | bytes 73760 | tf_op jit(solution)/shard_map/ppermute | solution.py:98
  32.4 0.0 copy-start.8
  32.4 0.0 collective-permute-done.2.refs_2_
  32.4 0.0 copy-start.2
  32.4 0.0 collective-permute-done.1.refs_1_
  32.4 0.0 copy-start.3
  32.4 0.0 collective-permute-done.refs_0_
  32.4 0.0 copy-start.4
  32.4 7.1 %all-to-all-start.1 = ((bf16[32,24,768]{2,1,0:T(8,128)(2,1)}), bf16[32,24,768]{2,1,0:T(8,128)(2,1)S(1)}, u32[]{:S(2)}, u32[]{:S(2)}) async-start(bf16[32,24,768]{2,1,0:T(8,128)(2,1)} %bitcast.3), calls=%async_computation.1 | async-start | bytes 2359296 | tf_op jit(solution)/shard_map/all_to_all | solution.py:252
  39.6 0.0 copy-done.4
  39.6 0.3 collective-permute-start.4
  39.9 0.0 copy-done.3
  39.9 0.3 collective-permute-start.5
  40.2 0.0 copy-done.2
  40.2 0.2 collective-permute-start.6
  40.4 0.0 copy-done.8
  40.4 0.3 collective-permute-start.7
  40.7 1.0 %collective-permute-done.7.refs_7_ = bf16[48,768]{1,0:T(8,128)(2,1)S(1)} collective-permute-done((bf16[48,768]{1,0:T(8,128)(2,1)S(1)}, bf16[48,768]{1,0:T(8,128)(2,1)S(1)}, u32[]{:S(2)}, u32[]{:S(2)}) %collective-permute-start.7) | collective-permute-done | bytes 73760 | tf_op jit(solution)/shard_map/ppermute | solution.py:104
  41.7 0.0 copy-start.9
  41.7 0.0 collective-permute-done.4.refs_4_
  41.7 0.0 copy-start.5
  41.7 0.0 collective-permute-done.5.refs_5_
  41.7 0.0 copy-start.6
  41.7 0.0 collective-permute-done.6.refs_6_
  41.7 0.0 copy-start.7
  41.8 0.6 copy-done.9
  42.3 0.1 copy-done.5
  42.4 0.0 copy-done.6
  42.4 0.1 copy-done.7
  42.5 12.9 %apply_virt.1.half_ref = bf16[48,256,768]{2,1,0:T(8,128)(2,1)} custom-call(bf16[6144,768]{1,0:T(8,128)(2,1)} %bitcast.10, s32[3,96]{1,0:T(4,128)} %occupancy_ref.3, bf16[96,768]{1,0:T(8,128)(2,1)} %bitcast.11, bf16[96,768]{1,0:T(8,128)(2,1)} %copy-done.4, bf16[96,768]{1,0:T(8,128)(2,1)} %copy-done.3, bf16[96,768]{1,0:T(8,128)(2,1)} %copy-done.2, ...), custom_call_target="tpu_custom_call" | custom-call | tf_op jit(solution)/shard_map/apply_virt/pallas_call | solution.py:144
  55.4 1.8 %all-to-all-done.1.returned_ref = bf16[32,24,768]{2,1,0:T(8,128)(2,1)S(1)} async-done(((bf16[32,24,768]{2,1,0:T(8,128)(2,1)}), bf16[32,24,768]{2,1,0:T(8,128)(2,1)S(1)}, u32[]{:S(2)}, u32[]{:S(2)}) %all-to-all-start.1) | async-done | bytes 1179680 | tf_op jit(solution)/shard_map/all_to_all | solution.py:252
  57.3 4.7 %contract.1 = f32[256,128]{1,0:T(8,128)S(1)} custom-call(bf16[32,24,768]{2,1,0:T(8,128)(2,1)S(1)} %all-to-all-done.1.returned_ref, bf16[48,256,768]{2,1,0:T(8,128)(2,1)} %apply_virt.1.half_ref), custom_call_target="tpu_custom_call" | custom-call | tf_op jit(solution)/shard_map/contract/pallas_call | solution.py:222
  62.0 13.0 %all_to_all.15 = f32[32,8,128]{2,1,0:T(8,128)S(1)} all-to-all(f32[32,8,128]{2,1,0:T(8,128)S(1)} %bitcast.9), channel_id=1, replica_groups=mesh['orb'=32,'aux'=8] {'orb'}, dimensions={0} | all-to-all | bytes 262144 | tf_op jit(solution)/shard_map/all_to_all | solution.py:255
  75.0 0.6 slice_reduce_fusion
  (1 shorter events, 0.0 us)
Async XLA Ops:
  2.1 8.8 %copy-start.1 = (bf16[768,96]{0,1:T(8,128)(2,1)S(1)}, bf16[768,96]{0,1:T(8,128)(2,1)}, u32[]{:S(2)}) copy-start(bf16[768,96]{0,1:T(8,128)(2,1)} %param.7) | copy-start | bytes 442372
  2.1 26.7 %copy-start = (bf16[768,768]{1,0:T(8,128)(2,1)S(1)}, bf16[768,768]{1,0:T(8,128)(2,1)}, u32[]{:S(2)}) copy-start(bf16[768,768]{1,0:T(8,128)(2,1)} %occ_ref.1) | copy-start | bytes 3538948
  2.2 26.7 %all-to-all-start = ((bf16[32,24,768]{2,1,0:T(8,128)(2,1)}), bf16[32,24,768]{2,1,0:T(8,128)(2,1)S(1)}, u32[]{:S(2)}, u32[]{:S(2)}) async-start(bf16[32,24,768]{2,1,0:T(8,128)(2,1)} %screen.1), calls=%async_computation | async-start | bytes 2359296 | tf_op jit(solution)/shard_map/all_to_all | solution.py:248
  10.9 21.5 %collective-permute-start.2 = (bf16[96,768]{1,0:T(8,128)(2,1)S(1)}, bf16[96,768]{1,0:T(8,128)(2,1)S(1)}, u32[]{:S(2)}, u32[]{:S(2)}) collective-permute-start(bf16[96,768]{1,0:T(8,128)(2,1)S(1)} %bitcast.12), channel_id=1, source_target_pairs={{0,5},{1,6},{2,7},{3,0},{4,1},{5,2},{6,3},{7,4},{8,11},{9,12},{10,... | collective-permute-start | bytes 442376 | tf_op jit(solution)/shard_map/ppermute | solution.py:98
  15.3 17.1 %collective-permute-start.1 = (bf16[96,768]{1,0:T(8,128)(2,1)S(1)}, bf16[96,768]{1,0:T(8,128)(2,1)S(1)}, u32[]{:S(2)}, u32[]{:S(2)}) collective-permute-start(bf16[96,768]{1,0:T(8,128)(2,1)S(1)} %bitcast.13), channel_id=1, source_target_pairs={{0,6},{1,7},{2,0},{3,1},{4,2},{5,3},{6,4},{7,5},{8,10},{9,11},{10,... | collective-permute-start | bytes 442376 | tf_op jit(solution)/shard_map/ppermute | solution.py:98
  18.6 13.8 %collective-permute-start = (bf16[96,768]{1,0:T(8,128)(2,1)S(1)}, bf16[96,768]{1,0:T(8,128)(2,1)S(1)}, u32[]{:S(2)}, u32[]{:S(2)}) collective-permute-start(bf16[96,768]{1,0:T(8,128)(2,1)S(1)} %bitcast.14), channel_id=1, source_target_pairs={{0,7},{1,0},{2,1},{3,2},{4,3},{5,4},{6,5},{7,6},{8,9},{9,10},{10,1... | collective-permute-start | bytes 442376 | tf_op jit(solution)/shard_map/ppermute | solution.py:98
  19.4 13.0 %collective-permute-start.3 = (bf16[48,768]{1,0:T(8,128)(2,1)S(1)}, bf16[48,768]{1,0:T(8,128)(2,1)S(1)}, u32[]{:S(2)}, u32[]{:S(2)}) collective-permute-start(bf16[48,768]{1,0:T(8,128)(2,1)S(1)} %dynamic-slice_bitcast_fusion), channel_id=1, source_target_pairs={{0,4},{1,5},{2,6},{3,7},{4,0},{5,1},{6,2},{7,3},{8,12},{9,13},{10,... | collective-permute-start | bytes 221192 | tf_op jit(solution)/shard_map/ppermute | solution.py:98
  32.4 8.1 %copy-start.8 = (bf16[48,768]{1,0:T(8,128)(2,1)}, bf16[48,768]{1,0:T(8,128)(2,1)S(1)}, u32[]{:S(2)}) copy-start(bf16[48,768]{1,0:T(8,128)(2,1)S(1)} %collective-permute-done.3.refs_3_) | copy-start | bytes 221188
  32.4 7.8 %copy-start.2 = (bf16[96,768]{1,0:T(8,128)(2,1)}, bf16[96,768]{1,0:T(8,128)(2,1)S(1)}, u32[]{:S(2)}) copy-start(bf16[96,768]{1,0:T(8,128)(2,1)S(1)} %collective-permute-done.2.refs_2_) | copy-start | bytes 442372
  32.4 7.5 %copy-start.3 = (bf16[96,768]{1,0:T(8,128)(2,1)}, bf16[96,768]{1,0:T(8,128)(2,1)S(1)}, u32[]{:S(2)}) copy-start(bf16[96,768]{1,0:T(8,128)(2,1)S(1)} %collective-permute-done.1.refs_1_) | copy-start | bytes 442372
  32.4 7.2 %copy-start.4 = (bf16[96,768]{1,0:T(8,128)(2,1)}, bf16[96,768]{1,0:T(8,128)(2,1)S(1)}, u32[]{:S(2)}) copy-start(bf16[96,768]{1,0:T(8,128)(2,1)S(1)} %collective-permute-done.refs_0_) | copy-start | bytes 442372
  32.4 24.8 %all-to-all-start.1 = ((bf16[32,24,768]{2,1,0:T(8,128)(2,1)}), bf16[32,24,768]{2,1,0:T(8,128)(2,1)S(1)}, u32[]{:S(2)}, u32[]{:S(2)}) async-start(bf16[32,24,768]{2,1,0:T(8,128)(2,1)} %bitcast.3), calls=%async_computation.1 | async-start | bytes 2359296 | tf_op jit(solution)/shard_map/all_to_all | solution.py:252
  39.6 2.1 %collective-permute-start.4 = (bf16[96,768]{1,0:T(8,128)(2,1)S(1)}, bf16[96,768]{1,0:T(8,128)(2,1)S(1)}, u32[]{:S(2)}, u32[]{:S(2)}) collective-permute-start(bf16[96,768]{1,0:T(8,128)(2,1)S(1)} %collective-permute-done.refs_0_), channel_id=1, source_target_pairs={{0,8},{8,0},{16,24},{24,16},{32,40},{40,32},{48,56},{56,48},{64,72... | collective-permute-start | bytes 442376 | tf_op jit(solution)/shard_map/ppermute | solution.py:104
  39.9 1.8 %collective-permute-start.5 = (bf16[96,768]{1,0:T(8,128)(2,1)S(1)}, bf16[96,768]{1,0:T(8,128)(2,1)S(1)}, u32[]{:S(2)}, u32[]{:S(2)}) collective-permute-start(bf16[96,768]{1,0:T(8,128)(2,1)S(1)} %collective-permute-done.1.refs_1_), channel_id=1, source_target_pairs={{0,8},{8,0},{16,24},{24,16},{32,40},{40,32},{48,56},{56,48},{64,72... | collective-permute-start | bytes 442376 | tf_op jit(solution)/shard_map/ppermute | solution.py:104
  40.2 1.5 %collective-permute-start.6 = (bf16[96,768]{1,0:T(8,128)(2,1)S(1)}, bf16[96,768]{1,0:T(8,128)(2,1)S(1)}, u32[]{:S(2)}, u32[]{:S(2)}) collective-permute-start(bf16[96,768]{1,0:T(8,128)(2,1)S(1)} %collective-permute-done.2.refs_2_), channel_id=1, source_target_pairs={{0,8},{8,0},{16,24},{24,16},{32,40},{40,32},{48,56},{56,48},{64,72... | collective-permute-start | bytes 442376 | tf_op jit(solution)/shard_map/ppermute | solution.py:104
  40.4 1.3 %collective-permute-start.7 = (bf16[48,768]{1,0:T(8,128)(2,1)S(1)}, bf16[48,768]{1,0:T(8,128)(2,1)S(1)}, u32[]{:S(2)}, u32[]{:S(2)}) collective-permute-start(bf16[48,768]{1,0:T(8,128)(2,1)S(1)} %collective-permute-done.3.refs_3_), channel_id=1, source_target_pairs={{0,8},{8,0},{16,24},{24,16},{32,40},{40,32},{48,56},{56,48},{64,72... | collective-permute-start | bytes 221192 | tf_op jit(solution)/shard_map/ppermute | solution.py:104
  41.7 0.6 copy-start.9
  41.7 0.7 copy-start.5
  41.7 0.7 copy-start.6
  41.7 0.8 copy-start.7

commit v5 on v4

--- a/solution.py
+++ b/solution.py
@@ -172,7 +172,7 @@
         copy.wait()
 
 
-def apply_occ(green_occ, screened, chunks=3):
+def apply_occ(green_occ, screened, chunks=2):
     return pl.pallas_call(
         apply_occ_kernel,
         in_specs=[VMEM] * 2,
@@ -215,7 +215,7 @@
         out_ref[:, :share] += total
 
 
-def contract(half_rows, returned, chunks=4):
+def contract(half_rows, returned, chunks=6):
     _, naux, cols = half_rows.shape
     share, rows, _ = returned.shape
     dtype = half_rows.dtype

time: 76 us -> 76.1 us (level)
  no operation moved by 1% of the time
where the time goes in v5:
time: 76.1 us; the launch traced here: 75.6 us
  starting transfers between devices  26 us (34%)
  Pallas kernels  21.8 us (29%)
  waiting for transfers between devices  13.4 us (18%)
  blocking collectives  13 us (17%)
  local copies, waits for them, and re-layouts  0.78 us (1%)
    all_to_all x1, blocking collectives, shards(): lax.all_to_all(parts, 'orb', split_axis=0, concat_axis=0, tiled=True)  13 us
    pallas_call x1, Pallas kernels, apply_virt(): pl.pallas_call(functools.partial(apply_virt_kernel, ranks), grid=(naux //...  12.9 us
    ppermute x4, starting transfers between devices, fetch_virt(): lax.ppermute(own if 2 * dist < ranks else own_half, ('orb', 'aux'), pairs)  9.01 us
    all_to_all x1, waiting for transfers between devices, shards(): lax.all_to_all(own, 'orb', split_axis=0, concat_axis=0, tiled=True)  8.96 us
    all_to_all x1, starting transfers between devices, shards(): lax.all_to_all(own, 'orb', split_axis=0, concat_axis=0, tiled=True)  8.73 us
    all_to_all x1, starting transfers between devices, shards(): lax.all_to_all(half_occ.reshape(ranks, mu_rows, nao), 'orb', split_axis=0...  7.15 us
    pallas_call x1, Pallas kernels, contract(): pl.pallas_call(contract_kernel, in_specs=[VMEM, ANY], out_specs=VMEM, out...  4.75 us
    pallas_call x1, Pallas kernels, screen(): pl.pallas_call(screen_kernel, in_specs=[ANY, ANY], out_specs=ANY, out_sha...  2.13 us
  transfers between devices with their start and end apart: 10, of which 4 were waited for; matrix products, arithmetic and copies ran while one was open for 0% of the time, Pallas kernels for 20%

profile of v5, /device:TPU:1, one launch (start us, length us, event | category | flops | bytes accessed | tf_op | source)
XLA Modules:
  0.0 75.6 jit_solution(14231434948136891321)
XLA Ops:
  0.0 2.1 %screen.1 = bf16[32,24,768]{2,1,0:T(8,128)(2,1)} custom-call(bf16[256,24,768]{2,1,0:T(8,128)(2,1)} %coulomb_ref.1, s32[3,96]{1,0:T(4,128)} %occupancy_ref.3), custom_call_target="tpu_custom_call" | custom-call | tf_op jit(solution)/shard_map/screen/pallas_call | solution.py:68
  2.1 0.0 copy-start.1
  2.1 0.0 copy-start
  2.2 8.7 %all-to-all-start = ((bf16[32,24,768]{2,1,0:T(8,128)(2,1)}), bf16[32,24,768]{2,1,0:T(8,128)(2,1)S(1)}, u32[]{:S(2)}, u32[]{:S(2)}) async-start(bf16[32,24,768]{2,1,0:T(8,128)(2,1)} %screen.1), calls=%async_computation | async-start | bytes 2359296 | tf_op jit(solution)/shard_map/all_to_all | solution.py:248
  10.9 0.0 copy-done.1
  10.9 4.4 %collective-permute-start.2 = (bf16[96,768]{1,0:T(8,128)(2,1)S(1)}, bf16[96,768]{1,0:T(8,128)(2,1)S(1)}, u32[]{:S(2)}, u32[]{:S(2)}) collective-permute-start(bf16[96,768]{1,0:T(8,128)(2,1)S(1)} %bitcast.12), channel_id=1, source_target_pairs={{0,5},{1,6},{2,7},{3,0},{4,1},{5,2},{6,3},{7,4},{8,11},{9,12},{10,... | collective-permute-start | bytes 442376 | tf_op jit(solution)/shard_map/ppermute | solution.py:98
  15.3 3.3 %collective-permute-start.1 = (bf16[96,768]{1,0:T(8,128)(2,1)S(1)}, bf16[96,768]{1,0:T(8,128)(2,1)S(1)}, u32[]{:S(2)}, u32[]{:S(2)}) collective-permute-start(bf16[96,768]{1,0:T(8,128)(2,1)S(1)} %bitcast.13), channel_id=1, source_target_pairs={{0,6},{1,7},{2,0},{3,1},{4,2},{5,3},{6,4},{7,5},{8,10},{9,11},{10,... | collective-permute-start | bytes 442376 | tf_op jit(solution)/shard_map/ppermute | solution.py:98
  18.6 0.7 collective-permute-start
  19.4 0.5 collective-permute-start.3
  19.9 9.0 %all-to-all-done = bf16[32,24,768]{2,1,0:T(8,128)(2,1)S(1)} async-done(((bf16[32,24,768]{2,1,0:T(8,128)(2,1)}), bf16[32,24,768]{2,1,0:T(8,128)(2,1)S(1)}, u32[]{:S(2)}, u32[]{:S(2)}) %all-to-all-start) | async-done | bytes 1179680 | tf_op jit(solution)/shard_map/all_to_all | solution.py:248
  28.9 0.0 copy-done
  28.9 1.9 %apply_occ.1 = bf16[768,768]{1,0:T(8,128)(2,1)} custom-call(bf16[768,768]{1,0:T(8,128)(2,1)S(1)} %copy-done, bf16[768,768]{1,0:T(8,128)(2,1)S(1)} %bitcast.8), custom_call_target="tpu_custom_call" | custom-call | tf_op jit(solution)/shard_map/apply_occ/pallas_call | solution.py:176
  30.8 1.6 %collective-permute-done.3.refs_3_ = bf16[48,768]{1,0:T(8,128)(2,1)S(1)} collective-permute-done((bf16[48,768]{1,0:T(8,128)(2,1)S(1)}, bf16[48,768]{1,0:T(8,128)(2,1)S(1)}, u32[]{:S(2)}, u32[]{:S(2)}) %collective-permute-start.3) | collective-permute-done | bytes 73760 | tf_op jit(solution)/shard_map/ppermute | solution.py:98
  32.4 0.0 copy-start.8
  32.4 0.0 collective-permute-done.2.refs_2_
  32.4 0.0 copy-start.2
  32.4 0.0 collective-permute-done.1.refs_1_
  32.4 0.0 copy-start.3
  32.4 0.0 collective-permute-done.refs_0_
  32.4 0.0 copy-start.4
  32.4 7.1 %all-to-all-start.1 = ((bf16[32,24,768]{2,1,0:T(8,128)(2,1)}), bf16[32,24,768]{2,1,0:T(8,128)(2,1)S(1)}, u32[]{:S(2)}, u32[]{:S(2)}) async-start(bf16[32,24,768]{2,1,0:T(8,128)(2,1)} %bitcast.3), calls=%async_computation.1 | async-start | bytes 2359296 | tf_op jit(solution)/shard_map/all_to_all | solution.py:252
  39.6 0.0 copy-done.4
  39.6 0.3 collective-permute-start.4
  39.9 0.0 copy-done.3
  39.9 0.3 collective-permute-start.5
  40.2 0.0 copy-done.2
  40.2 0.2 collective-permute-start.6
  40.4 0.0 copy-done.8
  40.4 0.3 collective-permute-start.7
  40.7 1.0 %collective-permute-done.7.refs_7_ = bf16[48,768]{1,0:T(8,128)(2,1)S(1)} collective-permute-done((bf16[48,768]{1,0:T(8,128)(2,1)S(1)}, bf16[48,768]{1,0:T(8,128)(2,1)S(1)}, u32[]{:S(2)}, u32[]{:S(2)}) %collective-permute-start.7) | collective-permute-done | bytes 73760 | tf_op jit(solution)/shard_map/ppermute | solution.py:104
  41.7 0.0 copy-start.9
  41.7 0.0 collective-permute-done.4.refs_4_
  41.7 0.0 copy-start.5
  41.7 0.0 collective-permute-done.5.refs_5_
  41.7 0.0 copy-start.6
  41.7 0.0 collective-permute-done.6.refs_6_
  41.7 0.0 copy-start.7
  41.8 0.6 copy-done.9
  42.3 0.1 copy-done.5
  42.4 0.0 copy-done.6
  42.4 0.1 copy-done.7
  42.5 12.9 %apply_virt.1.half_ref = bf16[48,256,768]{2,1,0:T(8,128)(2,1)} custom-call(bf16[6144,768]{1,0:T(8,128)(2,1)} %bitcast.10, s32[3,96]{1,0:T(4,128)} %occupancy_ref.3, bf16[96,768]{1,0:T(8,128)(2,1)} %bitcast.11, bf16[96,768]{1,0:T(8,128)(2,1)} %copy-done.4, bf16[96,768]{1,0:T(8,128)(2,1)} %copy-done.3, bf16[96,768]{1,0:T(8,128)(2,1)} %copy-done.2, ...), custom_call_target="tpu_custom_call" | custom-call | tf_op jit(solution)/shard_map/apply_virt/pallas_call | solution.py:144
  55.4 1.8 %all-to-all-done.1.returned_ref = bf16[32,24,768]{2,1,0:T(8,128)(2,1)S(1)} async-done(((bf16[32,24,768]{2,1,0:T(8,128)(2,1)}), bf16[32,24,768]{2,1,0:T(8,128)(2,1)S(1)}, u32[]{:S(2)}, u32[]{:S(2)}) %all-to-all-start.1) | async-done | bytes 1179680 | tf_op jit(solution)/shard_map/all_to_all | solution.py:252
  57.3 4.8 %contract.1 = f32[256,128]{1,0:T(8,128)S(1)} custom-call(bf16[32,24,768]{2,1,0:T(8,128)(2,1)S(1)} %all-to-all-done.1.returned_ref, bf16[48,256,768]{2,1,0:T(8,128)(2,1)} %apply_virt.1.half_ref), custom_call_target="tpu_custom_call" | custom-call | tf_op jit(solution)/shard_map/contract/pallas_call | solution.py:222
  62.0 13.0 %all_to_all.15 = f32[32,8,128]{2,1,0:T(8,128)S(1)} all-to-all(f32[32,8,128]{2,1,0:T(8,128)S(1)} %bitcast.9), channel_id=1, replica_groups=mesh['orb'=32,'aux'=8] {'orb'}, dimensions={0} | all-to-all | bytes 262144 | tf_op jit(solution)/shard_map/all_to_all | solution.py:255
  75.0 0.6 slice_reduce_fusion
  (1 shorter events, 0.0 us)
Async XLA Ops:
  2.1 8.8 %copy-start.1 = (bf16[768,96]{0,1:T(8,128)(2,1)S(1)}, bf16[768,96]{0,1:T(8,128)(2,1)}, u32[]{:S(2)}) copy-start(bf16[768,96]{0,1:T(8,128)(2,1)} %param.7) | copy-start | bytes 442372
  2.1 26.7 %copy-start = (bf16[768,768]{1,0:T(8,128)(2,1)S(1)}, bf16[768,768]{1,0:T(8,128)(2,1)}, u32[]{:S(2)}) copy-start(bf16[768,768]{1,0:T(8,128)(2,1)} %occ_ref.1) | copy-start | bytes 3538948
  2.2 26.7 %all-to-all-start = ((bf16[32,24,768]{2,1,0:T(8,128)(2,1)}), bf16[32,24,768]{2,1,0:T(8,128)(2,1)S(1)}, u32[]{:S(2)}, u32[]{:S(2)}) async-start(bf16[32,24,768]{2,1,0:T(8,128)(2,1)} %screen.1), calls=%async_computation | async-start | bytes 2359296 | tf_op jit(solution)/shard_map/all_to_all | solution.py:248
  10.9 21.5 %collective-permute-start.2 = (bf16[96,768]{1,0:T(8,128)(2,1)S(1)}, bf16[96,768]{1,0:T(8,128)(2,1)S(1)}, u32[]{:S(2)}, u32[]{:S(2)}) collective-permute-start(bf16[96,768]{1,0:T(8,128)(2,1)S(1)} %bitcast.12), channel_id=1, source_target_pairs={{0,5},{1,6},{2,7},{3,0},{4,1},{5,2},{6,3},{7,4},{8,11},{9,12},{10,... | collective-permute-start | bytes 442376 | tf_op jit(solution)/shard_map/ppermute | solution.py:98
  15.3 17.1 %collective-permute-start.1 = (bf16[96,768]{1,0:T(8,128)(2,1)S(1)}, bf16[96,768]{1,0:T(8,128)(2,1)S(1)}, u32[]{:S(2)}, u32[]{:S(2)}) collective-permute-start(bf16[96,768]{1,0:T(8,128)(2,1)S(1)} %bitcast.13), channel_id=1, source_target_pairs={{0,6},{1,7},{2,0},{3,1},{4,2},{5,3},{6,4},{7,5},{8,10},{9,11},{10,... | collective-permute-start | bytes 442376 | tf_op jit(solution)/shard_map/ppermute | solution.py:98
  18.6 13.8 %collective-permute-start = (bf16[96,768]{1,0:T(8,128)(2,1)S(1)}, bf16[96,768]{1,0:T(8,128)(2,1)S(1)}, u32[]{:S(2)}, u32[]{:S(2)}) collective-permute-start(bf16[96,768]{1,0:T(8,128)(2,1)S(1)} %bitcast.14), channel_id=1, source_target_pairs={{0,7},{1,0},{2,1},{3,2},{4,3},{5,4},{6,5},{7,6},{8,9},{9,10},{10,1... | collective-permute-start | bytes 442376 | tf_op jit(solution)/shard_map/ppermute | solution.py:98
  19.4 13.0 %collective-permute-start.3 = (bf16[48,768]{1,0:T(8,128)(2,1)S(1)}, bf16[48,768]{1,0:T(8,128)(2,1)S(1)}, u32[]{:S(2)}, u32[]{:S(2)}) collective-permute-start(bf16[48,768]{1,0:T(8,128)(2,1)S(1)} %dynamic-slice_bitcast_fusion), channel_id=1, source_target_pairs={{0,4},{1,5},{2,6},{3,7},{4,0},{5,1},{6,2},{7,3},{8,12},{9,13},{10,... | collective-permute-start | bytes 221192 | tf_op jit(solution)/shard_map/ppermute | solution.py:98
  32.4 8.1 %copy-start.8 = (bf16[48,768]{1,0:T(8,128)(2,1)}, bf16[48,768]{1,0:T(8,128)(2,1)S(1)}, u32[]{:S(2)}) copy-start(bf16[48,768]{1,0:T(8,128)(2,1)S(1)} %collective-permute-done.3.refs_3_) | copy-start | bytes 221188
  32.4 7.8 %copy-start.2 = (bf16[96,768]{1,0:T(8,128)(2,1)}, bf16[96,768]{1,0:T(8,128)(2,1)S(1)}, u32[]{:S(2)}) copy-start(bf16[96,768]{1,0:T(8,128)(2,1)S(1)} %collective-permute-done.2.refs_2_) | copy-start | bytes 442372
  32.4 7.5 %copy-start.3 = (bf16[96,768]{1,0:T(8,128)(2,1)}, bf16[96,768]{1,0:T(8,128)(2,1)S(1)}, u32[]{:S(2)}) copy-start(bf16[96,768]{1,0:T(8,128)(2,1)S(1)} %collective-permute-done.1.refs_1_) | copy-start | bytes 442372
  32.4 7.2 %copy-start.4 = (bf16[96,768]{1,0:T(8,128)(2,1)}, bf16[96,768]{1,0:T(8,128)(2,1)S(1)}, u32[]{:S(2)}) copy-start(bf16[96,768]{1,0:T(8,128)(2,1)S(1)} %collective-permute-done.refs_0_) | copy-start | bytes 442372
  32.4 24.8 %all-to-all-start.1 = ((bf16[32,24,768]{2,1,0:T(8,128)(2,1)}), bf16[32,24,768]{2,1,0:T(8,128)(2,1)S(1)}, u32[]{:S(2)}, u32[]{:S(2)}) async-start(bf16[32,24,768]{2,1,0:T(8,128)(2,1)} %bitcast.3), calls=%async_computation.1 | async-start | bytes 2359296 | tf_op jit(solution)/shard_map/all_to_all | solution.py:252
  39.6 2.1 %collective-permute-start.4 = (bf16[96,768]{1,0:T(8,128)(2,1)S(1)}, bf16[96,768]{1,0:T(8,128)(2,1)S(1)}, u32[]{:S(2)}, u32[]{:S(2)}) collective-permute-start(bf16[96,768]{1,0:T(8,128)(2,1)S(1)} %collective-permute-done.refs_0_), channel_id=1, source_target_pairs={{0,8},{8,0},{16,24},{24,16},{32,40},{40,32},{48,56},{56,48},{64,72... | collective-permute-start | bytes 442376 | tf_op jit(solution)/shard_map/ppermute | solution.py:104
  39.9 1.8 %collective-permute-start.5 = (bf16[96,768]{1,0:T(8,128)(2,1)S(1)}, bf16[96,768]{1,0:T(8,128)(2,1)S(1)}, u32[]{:S(2)}, u32[]{:S(2)}) collective-permute-start(bf16[96,768]{1,0:T(8,128)(2,1)S(1)} %collective-permute-done.1.refs_1_), channel_id=1, source_target_pairs={{0,8},{8,0},{16,24},{24,16},{32,40},{40,32},{48,56},{56,48},{64,72... | collective-permute-start | bytes 442376 | tf_op jit(solution)/shard_map/ppermute | solution.py:104
  40.2 1.5 %collective-permute-start.6 = (bf16[96,768]{1,0:T(8,128)(2,1)S(1)}, bf16[96,768]{1,0:T(8,128)(2,1)S(1)}, u32[]{:S(2)}, u32[]{:S(2)}) collective-permute-start(bf16[96,768]{1,0:T(8,128)(2,1)S(1)} %collective-permute-done.2.refs_2_), channel_id=1, source_target_pairs={{0,8},{8,0},{16,24},{24,16},{32,40},{40,32},{48,56},{56,48},{64,72... | collective-permute-start | bytes 442376 | tf_op jit(solution)/shard_map/ppermute | solution.py:104
  40.4 1.3 %collective-permute-start.7 = (bf16[48,768]{1,0:T(8,128)(2,1)S(1)}, bf16[48,768]{1,0:T(8,128)(2,1)S(1)}, u32[]{:S(2)}, u32[]{:S(2)}) collective-permute-start(bf16[48,768]{1,0:T(8,128)(2,1)S(1)} %collective-permute-done.3.refs_3_), channel_id=1, source_target_pairs={{0,8},{8,0},{16,24},{24,16},{32,40},{40,32},{48,56},{56,48},{64,72... | collective-permute-start | bytes 221192 | tf_op jit(solution)/shard_map/ppermute | solution.py:104
  41.7 0.6 copy-start.9
  41.7 0.7 copy-start.5
  41.7 0.7 copy-start.6
  41.7 0.8 copy-start.7

commit v6 on v4

--- a/solution.py
+++ b/solution.py
@@ -215,7 +215,7 @@
         out_ref[:, :share] += total
 
 
-def contract(half_rows, returned, chunks=4):
+def contract(half_rows, returned, chunks=3):
     _, naux, cols = half_rows.shape
     share, rows, _ = returned.shape
     dtype = half_rows.dtype

time: 76 us -> 76.1 us (level)
  no operation moved by 1% of the time
where the time goes in v6:
time: 76.1 us; the launch traced here: 75.7 us
  starting transfers between devices  26 us (34%)
  Pallas kernels  21.7 us (29%)
  waiting for transfers between devices  13.4 us (18%)
  blocking collectives  13 us (17%)
  local copies, waits for them, and re-layouts  0.78 us (1%)
    all_to_all x1, blocking collectives, shards(): lax.all_to_all(parts, 'orb', split_axis=0, concat_axis=0, tiled=True)  13 us
    pallas_call x1, Pallas kernels, apply_virt(): pl.pallas_call(functools.partial(apply_virt_kernel, ranks), grid=(naux //...  12.9 us
    ppermute x4, starting transfers between devices, fetch_virt(): lax.ppermute(own if 2 * dist < ranks else own_half, ('orb', 'aux'), pairs)  9.01 us
    all_to_all x1, waiting for transfers between devices, shards(): lax.all_to_all(own, 'orb', split_axis=0, concat_axis=0, tiled=True)  8.96 us
    all_to_all x1, starting transfers between devices, shards(): lax.all_to_all(own, 'orb', split_axis=0, concat_axis=0, tiled=True)  8.73 us
    all_to_all x1, starting transfers between devices, shards(): lax.all_to_all(half_occ.reshape(ranks, mu_rows, nao), 'orb', split_axis=0...  7.15 us
    pallas_call x1, Pallas kernels, contract(): pl.pallas_call(contract_kernel, in_specs=[VMEM, ANY], out_specs=VMEM, out...  4.8 us
    pallas_call x1, Pallas kernels, screen(): pl.pallas_call(screen_kernel, in_specs=[ANY, ANY], out_specs=ANY, out_sha...  2.13 us
  transfers between devices with their start and end apart: 10, of which 4 were waited for; matrix products, arithmetic and copies ran while one was open for 0% of the time, Pallas kernels for 20%

profile of v6, /device:TPU:1, one launch (start us, length us, event | category | flops | bytes accessed | tf_op | source)
XLA Modules:
  0.0 75.7 jit_solution(15836851545169715587)
XLA Ops:
  0.0 2.1 %screen.1 = bf16[32,24,768]{2,1,0:T(8,128)(2,1)} custom-call(bf16[256,24,768]{2,1,0:T(8,128)(2,1)} %coulomb_ref.1, s32[3,96]{1,0:T(4,128)} %occupancy_ref.3), custom_call_target="tpu_custom_call" | custom-call | tf_op jit(solution)/shard_map/screen/pallas_call | solution.py:68
  2.1 0.0 copy-start.1
  2.1 0.0 copy-start
  2.2 8.7 %all-to-all-start = ((bf16[32,24,768]{2,1,0:T(8,128)(2,1)}), bf16[32,24,768]{2,1,0:T(8,128)(2,1)S(1)}, u32[]{:S(2)}, u32[]{:S(2)}) async-start(bf16[32,24,768]{2,1,0:T(8,128)(2,1)} %screen.1), calls=%async_computation | async-start | bytes 2359296 | tf_op jit(solution)/shard_map/all_to_all | solution.py:248
  10.9 0.0 copy-done.1
  10.9 4.4 %collective-permute-start.2 = (bf16[96,768]{1,0:T(8,128)(2,1)S(1)}, bf16[96,768]{1,0:T(8,128)(2,1)S(1)}, u32[]{:S(2)}, u32[]{:S(2)}) collective-permute-start(bf16[96,768]{1,0:T(8,128)(2,1)S(1)} %bitcast.12), channel_id=1, source_target_pairs={{0,5},{1,6},{2,7},{3,0},{4,1},{5,2},{6,3},{7,4},{8,11},{9,12},{10,... | collective-permute-start | bytes 442376 | tf_op jit(solution)/shard_map/ppermute | solution.py:98
  15.3 3.3 %collective-permute-start.1 = (bf16[96,768]{1,0:T(8,128)(2,1)S(1)}, bf16[96,768]{1,0:T(8,128)(2,1)S(1)}, u32[]{:S(2)}, u32[]{:S(2)}) collective-permute-start(bf16[96,768]{1,0:T(8,128)(2,1)S(1)} %bitcast.13), channel_id=1, source_target_pairs={{0,6},{1,7},{2,0},{3,1},{4,2},{5,3},{6,4},{7,5},{8,10},{9,11},{10,... | collective-permute-start | bytes 442376 | tf_op jit(solution)/shard_map/ppermute | solution.py:98
  18.6 0.7 collective-permute-start
  19.4 0.5 collective-permute-start.3
  19.9 9.0 %all-to-all-done = bf16[32,24,768]{2,1,0:T(8,128)(2,1)S(1)} async-done(((bf16[32,24,768]{2,1,0:T(8,128)(2,1)}), bf16[32,24,768]{2,1,0:T(8,128)(2,1)S(1)}, u32[]{:S(2)}, u32[]{:S(2)}) %all-to-all-start) | async-done | bytes 1179680 | tf_op jit(solution)/shard_map/all_to_all | solution.py:248
  28.9 0.0 copy-done
  28.9 1.9 %apply_occ.1 = bf16[768,768]{1,0:T(8,128)(2,1)} custom-call(bf16[768,768]{1,0:T(8,128)(2,1)S(1)} %copy-done, bf16[768,768]{1,0:T(8,128)(2,1)S(1)} %bitcast.8), custom_call_target="tpu_custom_call" | custom-call | tf_op jit(solution)/shard_map/apply_occ/pallas_call | solution.py:176
  30.8 1.6 %collective-permute-done.3.refs_3_ = bf16[48,768]{1,0:T(8,128)(2,1)S(1)} collective-permute-done((bf16[48,768]{1,0:T(8,128)(2,1)S(1)}, bf16[48,768]{1,0:T(8,128)(2,1)S(1)}, u32[]{:S(2)}, u32[]{:S(2)}) %collective-permute-start.3) | collective-permute-done | bytes 73760 | tf_op jit(solution)/shard_map/ppermute | solution.py:98
  32.4 0.0 copy-start.8
  32.4 0.0 collective-permute-done.2.refs_2_
  32.4 0.0 copy-start.2
  32.4 0.0 collective-permute-done.1.refs_1_
  32.4 0.0 copy-start.3
  32.4 0.0 collective-permute-done.refs_0_
  32.4 0.0 copy-start.4
  32.4 7.1 %all-to-all-start.1 = ((bf16[32,24,768]{2,1,0:T(8,128)(2,1)}), bf16[32,24,768]{2,1,0:T(8,128)(2,1)S(1)}, u32[]{:S(2)}, u32[]{:S(2)}) async-start(bf16[32,24,768]{2,1,0:T(8,128)(2,1)} %bitcast.3), calls=%async_computation.1 | async-start | bytes 2359296 | tf_op jit(solution)/shard_map/all_to_all | solution.py:252
  39.6 0.0 copy-done.4
  39.6 0.3 collective-permute-start.4
  39.9 0.0 copy-done.3
  39.9 0.3 collective-permute-start.5
  40.2 0.0 copy-done.2
  40.2 0.2 collective-permute-start.6
  40.4 0.0 copy-done.8
  40.4 0.3 collective-permute-start.7
  40.7 1.0 %collective-permute-done.7.refs_7_ = bf16[48,768]{1,0:T(8,128)(2,1)S(1)} collective-permute-done((bf16[48,768]{1,0:T(8,128)(2,1)S(1)}, bf16[48,768]{1,0:T(8,128)(2,1)S(1)}, u32[]{:S(2)}, u32[]{:S(2)}) %collective-permute-start.7) | collective-permute-done | bytes 73760 | tf_op jit(solution)/shard_map/ppermute | solution.py:104
  41.7 0.0 copy-start.9
  41.7 0.0 collective-permute-done.4.refs_4_
  41.7 0.0 copy-start.5
  41.7 0.0 collective-permute-done.5.refs_5_
  41.7 0.0 copy-start.6
  41.7 0.0 collective-permute-done.6.refs_6_
  41.7 0.0 copy-start.7
  41.8 0.6 copy-done.9
  42.3 0.1 copy-done.5
  42.4 0.0 copy-done.6
  42.4 0.1 copy-done.7
  42.5 12.9 %apply_virt.1.half_ref = bf16[48,256,768]{2,1,0:T(8,128)(2,1)} custom-call(bf16[6144,768]{1,0:T(8,128)(2,1)} %bitcast.10, s32[3,96]{1,0:T(4,128)} %occupancy_ref.3, bf16[96,768]{1,0:T(8,128)(2,1)} %bitcast.11, bf16[96,768]{1,0:T(8,128)(2,1)} %copy-done.4, bf16[96,768]{1,0:T(8,128)(2,1)} %copy-done.3, bf16[96,768]{1,0:T(8,128)(2,1)} %copy-done.2, ...), custom_call_target="tpu_custom_call" | custom-call | tf_op jit(solution)/shard_map/apply_virt/pallas_call | solution.py:144
  55.4 1.8 %all-to-all-done.1.returned_ref = bf16[32,24,768]{2,1,0:T(8,128)(2,1)S(1)} async-done(((bf16[32,24,768]{2,1,0:T(8,128)(2,1)}), bf16[32,24,768]{2,1,0:T(8,128)(2,1)S(1)}, u32[]{:S(2)}, u32[]{:S(2)}) %all-to-all-start.1) | async-done | bytes 1179680 | tf_op jit(solution)/shard_map/all_to_all | solution.py:252
  57.3 4.8 %contract.1 = f32[256,128]{1,0:T(8,128)S(1)} custom-call(bf16[32,24,768]{2,1,0:T(8,128)(2,1)S(1)} %all-to-all-done.1.returned_ref, bf16[48,256,768]{2,1,0:T(8,128)(2,1)} %apply_virt.1.half_ref), custom_call_target="tpu_custom_call" | custom-call | tf_op jit(solution)/shard_map/contract/pallas_call | solution.py:222
  62.1 13.0 %all_to_all.15 = f32[32,8,128]{2,1,0:T(8,128)S(1)} all-to-all(f32[32,8,128]{2,1,0:T(8,128)S(1)} %bitcast.9), channel_id=1, replica_groups=mesh['orb'=32,'aux'=8] {'orb'}, dimensions={0} | all-to-all | bytes 262144 | tf_op jit(solution)/shard_map/all_to_all | solution.py:255
  75.0 0.6 slice_reduce_fusion
  (1 shorter events, 0.0 us)
Async XLA Ops:
  2.1 8.8 %copy-start.1 = (bf16[768,96]{0,1:T(8,128)(2,1)S(1)}, bf16[768,96]{0,1:T(8,128)(2,1)}, u32[]{:S(2)}) copy-start(bf16[768,96]{0,1:T(8,128)(2,1)} %param.7) | copy-start | bytes 442372
  2.1 26.7 %copy-start = (bf16[768,768]{1,0:T(8,128)(2,1)S(1)}, bf16[768,768]{1,0:T(8,128)(2,1)}, u32[]{:S(2)}) copy-start(bf16[768,768]{1,0:T(8,128)(2,1)} %occ_ref.1) | copy-start | bytes 3538948
  2.2 26.7 %all-to-all-start = ((bf16[32,24,768]{2,1,0:T(8,128)(2,1)}), bf16[32,24,768]{2,1,0:T(8,128)(2,1)S(1)}, u32[]{:S(2)}, u32[]{:S(2)}) async-start(bf16[32,24,768]{2,1,0:T(8,128)(2,1)} %screen.1), calls=%async_computation | async-start | bytes 2359296 | tf_op jit(solution)/shard_map/all_to_all | solution.py:248
  10.9 21.5 %collective-permute-start.2 = (bf16[96,768]{1,0:T(8,128)(2,1)S(1)}, bf16[96,768]{1,0:T(8,128)(2,1)S(1)}, u32[]{:S(2)}, u32[]{:S(2)}) collective-permute-start(bf16[96,768]{1,0:T(8,128)(2,1)S(1)} %bitcast.12), channel_id=1, source_target_pairs={{0,5},{1,6},{2,7},{3,0},{4,1},{5,2},{6,3},{7,4},{8,11},{9,12},{10,... | collective-permute-start | bytes 442376 | tf_op jit(solution)/shard_map/ppermute | solution.py:98
  15.3 17.1 %collective-permute-start.1 = (bf16[96,768]{1,0:T(8,128)(2,1)S(1)}, bf16[96,768]{1,0:T(8,128)(2,1)S(1)}, u32[]{:S(2)}, u32[]{:S(2)}) collective-permute-start(bf16[96,768]{1,0:T(8,128)(2,1)S(1)} %bitcast.13), channel_id=1, source_target_pairs={{0,6},{1,7},{2,0},{3,1},{4,2},{5,3},{6,4},{7,5},{8,10},{9,11},{10,... | collective-permute-start | bytes 442376 | tf_op jit(solution)/shard_map/ppermute | solution.py:98
  18.6 13.8 %collective-permute-start = (bf16[96,768]{1,0:T(8,128)(2,1)S(1)}, bf16[96,768]{1,0:T(8,128)(2,1)S(1)}, u32[]{:S(2)}, u32[]{:S(2)}) collective-permute-start(bf16[96,768]{1,0:T(8,128)(2,1)S(1)} %bitcast.14), channel_id=1, source_target_pairs={{0,7},{1,0},{2,1},{3,2},{4,3},{5,4},{6,5},{7,6},{8,9},{9,10},{10,1... | collective-permute-start | bytes 442376 | tf_op jit(solution)/shard_map/ppermute | solution.py:98
  19.4 13.0 %collective-permute-start.3 = (bf16[48,768]{1,0:T(8,128)(2,1)S(1)}, bf16[48,768]{1,0:T(8,128)(2,1)S(1)}, u32[]{:S(2)}, u32[]{:S(2)}) collective-permute-start(bf16[48,768]{1,0:T(8,128)(2,1)S(1)} %dynamic-slice_bitcast_fusion), channel_id=1, source_target_pairs={{0,4},{1,5},{2,6},{3,7},{4,0},{5,1},{6,2},{7,3},{8,12},{9,13},{10,... | collective-permute-start | bytes 221192 | tf_op jit(solution)/shard_map/ppermute | solution.py:98
  32.4 8.1 %copy-start.8 = (bf16[48,768]{1,0:T(8,128)(2,1)}, bf16[48,768]{1,0:T(8,128)(2,1)S(1)}, u32[]{:S(2)}) copy-start(bf16[48,768]{1,0:T(8,128)(2,1)S(1)} %collective-permute-done.3.refs_3_) | copy-start | bytes 221188
  32.4 7.8 %copy-start.2 = (bf16[96,768]{1,0:T(8,128)(2,1)}, bf16[96,768]{1,0:T(8,128)(2,1)S(1)}, u32[]{:S(2)}) copy-start(bf16[96,768]{1,0:T(8,128)(2,1)S(1)} %collective-permute-done.2.refs_2_) | copy-start | bytes 442372
  32.4 7.5 %copy-start.3 = (bf16[96,768]{1,0:T(8,128)(2,1)}, bf16[96,768]{1,0:T(8,128)(2,1)S(1)}, u32[]{:S(2)}) copy-start(bf16[96,768]{1,0:T(8,128)(2,1)S(1)} %collective-permute-done.1.refs_1_) | copy-start | bytes 442372
  32.4 7.2 %copy-start.4 = (bf16[96,768]{1,0:T(8,128)(2,1)}, bf16[96,768]{1,0:T(8,128)(2,1)S(1)}, u32[]{:S(2)}) copy-start(bf16[96,768]{1,0:T(8,128)(2,1)S(1)} %collective-permute-done.refs_0_) | copy-start | bytes 442372
  32.4 24.8 %all-to-all-start.1 = ((bf16[32,24,768]{2,1,0:T(8,128)(2,1)}), bf16[32,24,768]{2,1,0:T(8,128)(2,1)S(1)}, u32[]{:S(2)}, u32[]{:S(2)}) async-start(bf16[32,24,768]{2,1,0:T(8,128)(2,1)} %bitcast.3), calls=%async_computation.1 | async-start | bytes 2359296 | tf_op jit(solution)/shard_map/all_to_all | solution.py:252
  39.6 2.1 %collective-permute-start.4 = (bf16[96,768]{1,0:T(8,128)(2,1)S(1)}, bf16[96,768]{1,0:T(8,128)(2,1)S(1)}, u32[]{:S(2)}, u32[]{:S(2)}) collective-permute-start(bf16[96,768]{1,0:T(8,128)(2,1)S(1)} %collective-permute-done.refs_0_), channel_id=1, source_target_pairs={{0,8},{8,0},{16,24},{24,16},{32,40},{40,32},{48,56},{56,48},{64,72... | collective-permute-start | bytes 442376 | tf_op jit(solution)/shard_map/ppermute | solution.py:104
  39.9 1.8 %collective-permute-start.5 = (bf16[96,768]{1,0:T(8,128)(2,1)S(1)}, bf16[96,768]{1,0:T(8,128)(2,1)S(1)}, u32[]{:S(2)}, u32[]{:S(2)}) collective-permute-start(bf16[96,768]{1,0:T(8,128)(2,1)S(1)} %collective-permute-done.1.refs_1_), channel_id=1, source_target_pairs={{0,8},{8,0},{16,24},{24,16},{32,40},{40,32},{48,56},{56,48},{64,72... | collective-permute-start | bytes 442376 | tf_op jit(solution)/shard_map/ppermute | solution.py:104
  40.2 1.5 %collective-permute-start.6 = (bf16[96,768]{1,0:T(8,128)(2,1)S(1)}, bf16[96,768]{1,0:T(8,128)(2,1)S(1)}, u32[]{:S(2)}, u32[]{:S(2)}) collective-permute-start(bf16[96,768]{1,0:T(8,128)(2,1)S(1)} %collective-permute-done.2.refs_2_), channel_id=1, source_target_pairs={{0,8},{8,0},{16,24},{24,16},{32,40},{40,32},{48,56},{56,48},{64,72... | collective-permute-start | bytes 442376 | tf_op jit(solution)/shard_map/ppermute | solution.py:104
  40.4 1.3 %collective-permute-start.7 = (bf16[48,768]{1,0:T(8,128)(2,1)S(1)}, bf16[48,768]{1,0:T(8,128)(2,1)S(1)}, u32[]{:S(2)}, u32[]{:S(2)}) collective-permute-start(bf16[48,768]{1,0:T(8,128)(2,1)S(1)} %collective-permute-done.3.refs_3_), channel_id=1, source_target_pairs={{0,8},{8,0},{16,24},{24,16},{32,40},{40,32},{48,56},{56,48},{64,72... | collective-permute-start | bytes 221192 | tf_op jit(solution)/shard_map/ppermute | solution.py:104
  41.7 0.6 copy-start.9
  41.7 0.7 copy-start.5
  41.7 0.7 copy-start.6
  41.7 0.8 copy-start.7
